TPU v7x, 512 devices: a whole 4x8x8 slice. The times are simulated.
512 devices in a mesh: seq: 32 (over z, x), mem: 16 (over y, core).
Axes of the slice: x: 4, y: 8, z: 8, core: 2. Of those that a mesh axis runs over, the one named last changes fastest.
Arguments:
- queries: bfloat16 [65536, 2048], P(('seq', 'mem')), may hold values from -6 to 6
- keys: bfloat16 [65536, 2048], P(('seq', 'mem')), may hold values from -0.52734375 to 0.52734375
- values: bfloat16 [65536, 2048], P(('seq', 'mem')), may hold values from -6 to 6
- gamma: bfloat16 [65536, 16], P(('seq', 'mem')), as said below
- rate: bfloat16 [16, 16], replicated, as said below
- route_ids: int32 [65536, 2], P(('seq', 'mem')), may hold values from 0 to 15, all different within a row; in each aligned block of 128 rows (0 to 127, 128 to 255, ...) at most 24 rows name the same one
- route_weights: float32 [65536, 2], P(('seq', 'mem')), may hold values from 0.2 to 1
- norm_gain: float32 [2048], replicated, may hold values from 0.25 to 1.75
Outputs:
- mixed_out: bfloat16 [65536, 2048], P(('seq', 'mem'))
Inputs may be any that keep to these rules, and one draw needn't show every extreme that they name: `route_ids`: each token names two different memories. The tokens of one device name one memory at most 24 times; some memory is named exactly 24 times by some device's tokens. `gamma`: Positive; from 0.5 up to 24576. `rate`: Positive; from 0.04 * 16 / 65536 up to 0.06.
All inputs are finite; a program needn't handle non-finite values.
Results may differ from a plain program's by a relative error of at most 0.0052.
Values may be sent and summed in bfloat16 or wider, within the bound.
No kernel may reach another device: no remote copies, remote signals or barrier semaphores. Data moves between devices by JAX's collectives and lax.ppermute only.
A program may use at most 128 MiB of HBM per device.

v0:
```python
import jax
import jax.numpy as jnp
from jax import lax
from jax.sharding import Mesh
from jax.sharding import PartitionSpec as P

BLOCK = 128
SEQ = ("seq_0", "seq_1")
SEQ_MEM = ("seq_0", "seq_1", "mem")


epsilon = 1e-06


def nothing_yet(x, identity):
    return jax.tree.map(
        lambda part, zero: jnp.zeros_like(part) + jnp.asarray(zero, part.dtype), x, identity
    )


def prefix_by_axis(x, axes, combine, identity):
    before = start = nothing_yet(x, identity)
    total = x
    for axis in reversed(axes):
        peers, position = (lax.axis_size(axis), lax.axis_index(axis))
        pieces = jax.tree.map(lambda part: lax.all_gather(part, axis), total)
        inside, total = (start, start)
        for k in range(peers):
            passed = k < position
            total = combine(total, jax.tree.map(lambda part: part[k], pieces))
            inside = jax.tree.map(lambda new, old: jnp.where(passed, new, old), total, inside)
        before = combine(inside, before)
    return before


def combine_state(earlier, later_part):
    return (earlier[0] * later_part[0], later_part[0][:, None, None] * earlier[1] + later_part[1])


def owner_heads(query_rows, key_rows, value_rows, gamma_rows, rate_rows):
    sources, capacity, head_count, head_width = query_rows.shape
    block_count = sources * capacity // BLOCK
    query_rows = query_rows.reshape(block_count, BLOCK, head_count, head_width)
    key_rows = key_rows.reshape(block_count, BLOCK, head_count, head_width)
    value_rows = value_rows.reshape(block_count, BLOCK, head_count, head_width)
    rate_now = rate_rows[0, 0].astype(jnp.float32)
    levels = jnp.cumsum(
        -rate_now[None, None, :]
        * gamma_rows.reshape(block_count, BLOCK, head_count).astype(jnp.float32),
        axis=1,
    )
    spread_log = levels[:, :, None, :] - levels[:, None, :, :]
    causal = (jnp.arange(BLOCK)[:, None] >= jnp.arange(BLOCK)[None, :])[None, :, :, None]
    decays = jnp.exp(jnp.where(causal, spread_log, -1e30))
    scores = jnp.einsum("bthd,bshd->btsh", query_rows, key_rows, preferred_element_type=jnp.float32)
    weights = (decays * scores).astype(jnp.bfloat16)
    intra_out = jnp.einsum(
        "btsh,bshe->bthe", weights, value_rows, preferred_element_type=jnp.float32
    )
    last_level = levels[:, -1, :]
    keyed_rows = (
        key_rows.astype(jnp.float32) * jnp.exp(last_level[:, None, :] - levels)[..., None]
    ).astype(jnp.bfloat16)
    updates = jnp.einsum(
        "bshd,bshe->bhde", keyed_rows, value_rows, preferred_element_type=jnp.float32
    )
    fading = jnp.exp(last_level)

    def local_step(carried, inputs_now):
        fade_now, update_now = inputs_now
        next_carry = (carried[0] * fade_now, fade_now[:, None, None] * carried[1] + update_now)
        return (next_carry, carried)

    start_fade = jnp.ones((head_count,), jnp.float32)
    start_state = jnp.zeros((head_count, head_width, head_width), jnp.float32)
    device_sum, entering = lax.scan(local_step, (start_fade, start_state), (fading, updates))
    before_fade, before_state = prefix_by_axis(
        device_sum, SEQ, combine_state, (start_fade, start_state)
    )
    states = entering[1] + entering[0][:, :, None, None] * before_state[None]
    scaled_query = query_rows.astype(jnp.float32) * jnp.exp(levels)[..., None]
    inter_out = jnp.einsum("bthd,bhde->bthe", scaled_query, states, precision=lax.Precision.HIGHEST)
    raw_out = intra_out + inter_out
    normed = raw_out * lax.rsqrt(jnp.mean(raw_out * raw_out, axis=-1, keepdims=True) + epsilon)
    return normed.astype(jnp.bfloat16).reshape(sources, capacity, head_count, head_width)


def body(queries, keys, values, gamma, rate, route_ids, route_weights, norm_gain):
    token_count, feat_count = queries.shape
    head_count = gamma.shape[1]
    head_width = feat_count // head_count
    owners = lax.axis_size("mem")
    capacity = 3 * token_count // owners
    flat_routes = route_ids.reshape(-1)
    route_hits = (flat_routes[:, None] == jnp.arange(owners, dtype=jnp.int32)[None, :]).astype(
        jnp.int32
    )
    earlier_hits = jnp.cumsum(route_hits, axis=0) - route_hits
    route_rank = jnp.sum(route_hits * earlier_hits, axis=1)
    slot_ids = (flat_routes * capacity + route_rank).reshape(token_count, 2)
    slot_range = jnp.arange(owners * capacity, dtype=jnp.int32)
    chosen = (slot_ids[:, 0][None, :] == slot_range[:, None]) | (
        slot_ids[:, 1][None, :] == slot_range[:, None]
    )
    select = chosen.astype(jnp.bfloat16)

    def place_rows(row_block):
        return jnp.dot(select, row_block, preferred_element_type=jnp.float32).astype(jnp.bfloat16)

    send_query = place_rows(queries).reshape(owners, capacity, head_count, head_width)
    send_key = place_rows(keys).reshape(owners, capacity, head_count, head_width)
    send_value = place_rows(values).reshape(owners, capacity, head_count, head_width)
    send_gamma = place_rows(gamma).reshape(owners, capacity, head_count)
    send_rate = rate[:, None, :]
    arrived = (
        lax.all_to_all(send_query, "mem", split_axis=0, concat_axis=0, tiled=True),
        lax.all_to_all(send_key, "mem", split_axis=0, concat_axis=0, tiled=True),
        lax.all_to_all(send_value, "mem", split_axis=0, concat_axis=0, tiled=True),
        lax.all_to_all(send_gamma, "mem", split_axis=0, concat_axis=0, tiled=True),
        lax.all_to_all(send_rate, "mem", split_axis=0, concat_axis=0, tiled=True),
    )
    returned = lax.all_to_all(owner_heads(*arrived), "mem", split_axis=0, concat_axis=0, tiled=True)
    returned = returned.reshape(owners * capacity, feat_count)
    pick_first = (slot_ids[:, 0][:, None] == slot_range[None, :]).astype(jnp.bfloat16)
    pick_second = (slot_ids[:, 1][:, None] == slot_range[None, :]).astype(jnp.bfloat16)
    first_out = jnp.dot(pick_first, returned, preferred_element_type=jnp.float32)
    second_out = jnp.dot(pick_second, returned, preferred_element_type=jnp.float32)
    mixed_out = norm_gain[None, :] * (
        route_weights[:, 0:1] * first_out + route_weights[:, 1:2] * second_out
    )
    return mixed_out.astype(jnp.bfloat16)


def solution(mesh):
    split = Mesh(mesh.devices.reshape(8, 4, mesh.shape["mem"]), ("seq_0", "seq_1", "mem"))
    in_specs = (
        P(SEQ_MEM, None),
        P(SEQ_MEM, None),
        P(SEQ_MEM, None),
        P(SEQ_MEM, None),
        P(),
        P(SEQ_MEM, None),
        P(SEQ_MEM, None),
        P(),
    )
    out_specs = P(SEQ_MEM, None)
    return jax.shard_map(body, mesh=split, in_specs=in_specs, out_specs=out_specs, check_vma=False)
```

profile of v0, /device:TPU:1, one launch (start us, length us, event | category | flops | bytes accessed | tf_op | source)
XLA Modules:
  0.0 374.5 jit_solution(4329417801561947873)
XLA Ops:
  6.5 1.3 copy.82
  7.9 10.1 %all-to-all-start.1 = ((bf16[16,1,16]{2,1,0:T(2,128)(2,1)}), bf16[16,1,16]{2,1,0:T(2,128)(2,1)S(1)}, u32[]{:S(2)}, u32[]{:S(2)}) async-start(bf16[16,1,16]{2,1,0:T(2,128)(2,1)} %copy.82), calls=%async_computation.1 | async-start | bytes 16384 | tf_op jit(solution)/shard_map/all_to_all | solution.py:120
  18.0 0.8 copy.78
  20.2 0.7 multiply_add_fusion
  20.9 0.8 convolution_convert_fusion.3
  21.9 0.7 reshape.182
  22.7 2.4 all-to-all-done.1
  25.0 4.9 %all-to-all-start.2 = ((bf16[16,2,192]{2,1,0:T(2,128)(2,1)}), bf16[16,2,192]{2,1,0:T(2,128)(2,1)S(1)}, u32[]{:S(2)}, u32[]{:S(2)}) async-start(bf16[16,2,192]{2,1,0:T(2,128)(2,1)} %reshape.182), calls=%async_computation.2 | async-start | bytes 32768 | tf_op jit(solution)/shard_map/all_to_all | solution.py:119
  30.5 1.6 copy.100
  32.1 5.1 %all-to-all-done.2 = bf16[16,2,192]{2,1,0:T(2,128)(2,1)S(1)} async-done(((bf16[16,2,192]{2,1,0:T(2,128)(2,1)}), bf16[16,2,192]{2,1,0:T(2,128)(2,1)S(1)}, u32[]{:S(2)}, u32[]{:S(2)}) %all-to-all-start.2) | async-done | bytes 12320 | tf_op jit(solution)/shard_map/all_to_all | solution.py:119
  37.3 3.9 %all-to-all-start.3 = ((bf16[16,24,16,128]{3,2,1,0:T(8,128)(2,1)}), bf16[16,24,16,128]{3,2,1,0:T(8,128)(2,1)S(1)}, u32[]{:S(2)}, u32[]{:S(2)}) async-start(bf16[16,24,16,128]{3,2,1,0:T(8,128)(2,1)} %bitcast.165), calls=%async_computation.3 | async-start | bytes 3145728 | tf_op jit(solution)/shard_map/all_to_all | solution.py:117
  41.7 1.6 copy.99
  43.3 36.4 %all-to-all-done.3 = bf16[16,24,16,128]{3,2,1,0:T(8,128)(2,1)S(1)} async-done(((bf16[16,24,16,128]{3,2,1,0:T(8,128)(2,1)}), bf16[16,24,16,128]{3,2,1,0:T(8,128)(2,1)S(1)}, u32[]{:S(2)}, u32[]{:S(2)}) %all-to-all-start.3) | async-done | bytes 1572896 | tf_op jit(solution)/shard_map/all_to_all | solution.py:117
  79.6 4.3 %all-to-all-start = ((bf16[16,24,16,128]{3,2,1,0:T(8,128)(2,1)}), bf16[16,24,16,128]{3,2,1,0:T(8,128)(2,1)}, u32[]{:S(2)}, u32[]{:S(2)}) async-start(bf16[16,24,16,128]{3,2,1,0:T(8,128)(2,1)} %bitcast.164), calls=%async_computation | async-start | bytes 3145728 | tf_op jit(solution)/shard_map/all_to_all | solution.py:118
  85.4 1.9 multiply_convert_fusion
  87.2 35.2 %all-to-all-done = bf16[16,24,16,128]{3,2,1,0:T(8,128)(2,1)} async-done(((bf16[16,24,16,128]{3,2,1,0:T(8,128)(2,1)}), bf16[16,24,16,128]{3,2,1,0:T(8,128)(2,1)}, u32[]{:S(2)}, u32[]{:S(2)}) %all-to-all-start) | async-done | bytes 1572896 | tf_op jit(solution)/shard_map/all_to_all | solution.py:118
  122.4 4.3 %fusion.15 = f32[3,16,128,128]{3,2,1,0:T(8,128)} fusion(bf16[3,128,16,128]{3,2,1,0:T(8,128)(2,1)} %multiply_convert_fusion, bf16[3,128,16,128]{3,2,1,0:T(8,128)(2,1)} %bitcast.4), kind=kOutput, calls=%fused_computation.30 | convolution fusion | flops 201326592 | bytes 6291456 | tf_op jit(solution)/shard_map/bshd,bshe->bhde/dot_general | solution.py:64
  126.7 13.4 %while.17 = (s32[]{:T(128)}, f32[16]{0:T(128)S(1)}, f32[16,128,128]{2,1,0:T(8,128)S(1)}, f32[3,16]{1,0:T(4,128)}, f32[3,16,128,128]{3,2,1,0:T(8,128)}, /*index=5...) while((s32[]{:T(128)}, f32[16]{0:T(128)S(1)}, ...), condition=%wide.region_5.6_spmd.clone, body=%wide.region_4.5_spmd.clone.sunk | while | flops 1048611 | bytes 5244021 | solution.py:76
  126.7 0.7 fusion.66
  127.4 1.1 bitcast_dynamic-update-slice_fusion.2
  128.5 1.4 bitcast_add_fusion.2
  129.9 1.3 dynamic_update_slice.14
  131.2 0.7 fusion.66
  131.9 1.1 bitcast_dynamic-update-slice_fusion.2
  132.9 1.4 bitcast_add_fusion.2
  134.3 1.3 dynamic_update_slice.14
  136.3 1.1 bitcast_dynamic-update-slice_fusion.2
  137.4 1.4 bitcast_add_fusion.2
  138.8 1.3 dynamic_update_slice.14
  140.1 1.0 copy-done.1
  141.1 1.3 dynamic-slice
  143.2 7.2 %all-reduce = f32[64]{0:T(128)S(1)} all-reduce(f32[64]{0:T(128)S(1)} %dynamic-update-slice), channel_id=2, replica_groups=mesh['seq_0'=8,'seq_1'=4,'mem'=16] {'seq_1'}, use_global_device_ids=true, to_apply=%add | all-reduce | flops 64 | bytes 512
  150.5 43.9 %all-gather.8.cloned.1.call-done = f32[64,128,128]{2,1,0:T(8,128)} async-done(((f32[16,128,128]{2,1,0:T(8,128)}), f32[64,128,128]{2,1,0:T(8,128)}) %all-gather.8.cloned.1.call-update) | async-done | bytes 4194320 | tf_op jit(solution)/shard_map/all_gather | solution.py:26
  194.4 3.7 fusion.36
  198.7 1.6 copy.101
  200.2 7.4 %all-to-all-start.4 = ((bf16[16,24,16,128]{3,2,1,0:T(8,128)(2,1)}), bf16[16,24,16,128]{3,2,1,0:T(8,128)(2,1)}, u32[]{:S(2)}, u32[]{:S(2)}) async-start(bf16[16,24,16,128]{3,2,1,0:T(8,128)(2,1)} %bitcast.163), calls=%async_computation.4 | async-start | bytes 3145728 | tf_op jit(solution)/shard_map/all_to_all | solution.py:116
  207.7 14.4 %all-gather.2 = f32[8,1,16]{2,1,0:T(1,128)S(1)} all-gather(f32[1,1,16]{2,1,0:T(1,128)S(1)} %get-tuple-element.106), channel_id=1, replica_groups=mesh['seq_0'=8,'seq_1'=4,'mem'=16] {'seq_0'}, dimensions={0}, use_global_device_ids=true | all-gather | bytes 576 | tf_op jit(solution)/shard_map/all_gather | solution.py:26
  222.1 24.1 %all-to-all-done.4 = bf16[16,24,16,128]{3,2,1,0:T(8,128)(2,1)} async-done(((bf16[16,24,16,128]{3,2,1,0:T(8,128)(2,1)}), bf16[16,24,16,128]{3,2,1,0:T(8,128)(2,1)}, u32[]{:S(2)}, u32[]{:S(2)}) %all-to-all-start.4) | async-done | bytes 1572896 | tf_op jit(solution)/shard_map/all_to_all | solution.py:116
  246.2 3.3 convert_multiply_fusion
  249.5 46.7 %all-gather.6.cloned.1.call-done = f32[8,16,128,128]{3,2,1,0:T(8,128)} async-done(((f32[1,16,128,128]{3,2,1,0:T(8,128)}), f32[8,16,128,128]{3,2,1,0:T(8,128)}) %all-gather.6.cloned.1.call-update) | async-done | bytes 8388624 | tf_op jit(solution)/shard_map/all_gather | solution.py:26
  296.2 6.0 %fusion.35 = f32[16,128,128]{2,1,0:T(8,128)S(1)} fusion(f32[8,16,128,128]{3,2,1,0:T(8,128)} %all-gather.6.cloned.1.call-done, f32[64,128,128]{2,1,0:T(8,128)} %all-gather.8.cloned.1.call-done, f32[16]{0:T(128)S(1)} %get-tuple-element.105, f32[16]{0:T(128)S(1)} %get-tuple-element.109, f32[16]{0:T(128)S(1)} %get-tuple-element.99, f32[16]{0:T(128)S(1)} %get-tuple-element.93, ...), kind=kLoop, calls=%fused_computation.48 | loop fusion | flops 9437184 | bytes 13632332 | tf_op jit(solution)/shard_map/mul | solution.py:80
  302.7 5.6 %fusion.6 = f32[3,16,128,128]{2,3,1,0:T(8,128)} fusion(f32[3,128,16,128]{3,2,1,0:T(8,128)S(1)} %copy-done.2, f32[3,16,128,128]{3,2,1,0:T(8,128)S(1)} %copy-done.3, f32[16,128,128]{2,1,0:T(8,128)S(1)} %fusion.35, f32[3,16]{1,0:T(4,128)S(1)} %copy-done.7), kind=kOutput, calls=%fused_computation.13 | convolution fusion | flops 1209532416 | bytes 10485952 | tf_op jit(solution)/shard_map/bthd,bhde->bthe/dot_general | solution.py:82
  308.4 6.8 %fusion.3 = (f32[3,128,16]{1,2,0:T(8,128)S(1)}, f32[3,16,128,128]{2,3,1,0:T(8,128)}) fusion(f32[3,16,128,128]{2,3,1,0:T(8,128)} %fusion.6, bf16[3,128,16,128]{3,2,1,0:T(8,128)(2,1)} %bitcast.8, bf16[3,128,16,128]{3,2,1,0:T(8,128)(2,1)S(1)} %bitcast.162, f32[3,128,16]{1,2,0:T(8,128)S(1)} %copy.86, pred[128,128]{0,1:T(8,128)(4,1)S(1)} %iota_compare_fusion.6, ...), kind=kOutput, calls=%fused_computation.9 | convolution fusion | flops 408152064 | bytes 11075584 | tf_op jit(solution)/shard_map/btsh,bshe->bthe/dot_general | solution.py:57
  315.2 2.4 fusion.4
  317.6 2.2 copy.95
  319.8 7.6 %all-to-all-start.5 = ((bf16[16,24,16,128]{3,2,1,0:T(8,128)(2,1)}), bf16[16,24,16,128]{3,2,1,0:T(8,128)(2,1)S(1)}, u32[]{:S(2)}, u32[]{:S(2)}) async-start(bf16[16,24,16,128]{3,2,1,0:T(8,128)(2,1)} %bitcast.166), calls=%async_computation.5 | async-start | bytes 3145728 | tf_op jit(solution)/shard_map/all_to_all | solution.py:122
  327.4 38.4 %all-to-all-done.5 = bf16[16,24,16,128]{3,2,1,0:T(8,128)(2,1)S(1)} async-done(((bf16[16,24,16,128]{3,2,1,0:T(8,128)(2,1)}), bf16[16,24,16,128]{3,2,1,0:T(8,128)(2,1)S(1)}, u32[]{:S(2)}, u32[]{:S(2)}) %all-to-all-start.5) | async-done | bytes 1572896 | tf_op jit(solution)/shard_map/all_to_all | solution.py:122
  366.3 1.3 fusion.12
  (62 shorter events, 6.7 us)
Async XLA Ops:
  6.5 23.4 %copy-start = (bf16[128,2048]{1,0:T(8,128)(2,1)S(1)}, bf16[128,2048]{1,0:T(8,128)(2,1)}, u32[]{:S(2)}) copy-start(bf16[128,2048]{1,0:T(8,128)(2,1)} %param.11) | copy-start | bytes 1572868
  7.9 17.2 %all-to-all-start.1 = ((bf16[16,1,16]{2,1,0:T(2,128)(2,1)}), bf16[16,1,16]{2,1,0:T(2,128)(2,1)S(1)}, u32[]{:S(2)}, u32[]{:S(2)}) async-start(bf16[16,1,16]{2,1,0:T(2,128)(2,1)} %copy.82), calls=%async_computation.1 | async-start | bytes 16384 | tf_op jit(solution)/shard_map/all_to_all | solution.py:120
  25.0 12.2 %all-to-all-start.2 = ((bf16[16,2,192]{2,1,0:T(2,128)(2,1)}), bf16[16,2,192]{2,1,0:T(2,128)(2,1)S(1)}, u32[]{:S(2)}, u32[]{:S(2)}) async-start(bf16[16,2,192]{2,1,0:T(2,128)(2,1)} %reshape.182), calls=%async_computation.2 | async-start | bytes 32768 | tf_op jit(solution)/shard_map/all_to_all | solution.py:119
  30.5 10.6 %copy-start.4 = (bf16[128,2048]{1,0:T(8,128)(2,1)S(1)}, bf16[128,2048]{1,0:T(8,128)(2,1)}, u32[]{:S(2)}) copy-start(bf16[128,2048]{1,0:T(8,128)(2,1)} %param.12) | copy-start | bytes 1572868
  37.3 42.4 %all-to-all-start.3 = ((bf16[16,24,16,128]{3,2,1,0:T(8,128)(2,1)}), bf16[16,24,16,128]{3,2,1,0:T(8,128)(2,1)S(1)}, u32[]{:S(2)}, u32[]{:S(2)}) async-start(bf16[16,24,16,128]{3,2,1,0:T(8,128)(2,1)} %bitcast.165), calls=%async_computation.3 | async-start | bytes 3145728 | tf_op jit(solution)/shard_map/all_to_all | solution.py:117
  79.6 42.8 %all-to-all-start = ((bf16[16,24,16,128]{3,2,1,0:T(8,128)(2,1)}), bf16[16,24,16,128]{3,2,1,0:T(8,128)(2,1)}, u32[]{:S(2)}, u32[]{:S(2)}) async-start(bf16[16,24,16,128]{3,2,1,0:T(8,128)(2,1)} %bitcast.164), calls=%async_computation | async-start | bytes 3145728 | tf_op jit(solution)/shard_map/all_to_all | solution.py:118
  83.9 110.5 %all-gather.8.cloned.1.call-start = ((), (), s32[]{:S(2)}) async-start(), calls=%async_computation.7 | async-start | bytes 5242880 | tf_op jit(solution)/shard_map/all_gather | solution.py:26
  140.1 1.0 copy-start.1
  141.1 155.2 %all-gather.6.cloned.1.call-start = ((), (), s32[]{:S(2)}) async-start(), calls=%async_computation.6 | async-start | bytes 9437184 | tf_op jit(solution)/shard_map/all_gather | solution.py:26
  194.4 3.7 copy-start.5
  200.2 46.0 %all-to-all-start.4 = ((bf16[16,24,16,128]{3,2,1,0:T(8,128)(2,1)}), bf16[16,24,16,128]{3,2,1,0:T(8,128)(2,1)}, u32[]{:S(2)}, u32[]{:S(2)}) async-start(bf16[16,24,16,128]{3,2,1,0:T(8,128)(2,1)} %bitcast.163), calls=%async_computation.4 | async-start | bytes 3145728 | tf_op jit(solution)/shard_map/all_to_all | solution.py:116
  296.2 6.1 %copy-start.2 = (f32[3,128,16,128]{3,2,1,0:T(8,128)S(1)}, f32[3,128,16,128]{3,2,1,0:T(8,128)}, u32[]{:S(2)}) copy-start(f32[3,128,16,128]{3,2,1,0:T(8,128)} %convert_multiply_fusion) | copy-start | bytes 9437188
  296.2 6.5 %copy-start.3 = (f32[3,16,128,128]{3,2,1,0:T(8,128)S(1)}, f32[3,16,128,128]{3,2,1,0:T(8,128)}, u32[]{:S(2)}) copy-start(f32[3,16,128,128]{3,2,1,0:T(8,128)} %get-tuple-element.45) | copy-start | bytes 9437188
  296.2 6.5 %copy-start.7 = (f32[3,16]{1,0:T(4,128)S(1)}, f32[3,16]{1,0:T(4,128)}, u32[]{:S(2)}) copy-start(f32[3,16]{1,0:T(4,128)} %get-tuple-element.46) | copy-start | bytes 580
  317.6 9.8 %copy-start.8 = (f32[128,2]{0,1:T(2,128)S(1)}, f32[128,2]{0,1:T(2,128)}, u32[]{:S(2)}) copy-start(f32[128,2]{0,1:T(2,128)} %param.16) | copy-start | bytes 3076
  319.8 46.5 %copy-start.6 = (f32[2048]{0:T(1024)S(1)}, f32[2048]{0:T(1024)}, u32[]{:S(2)}) copy-start(f32[2048]{0:T(1024)} %param.17) | copy-start | bytes 24580
  319.8 46.0 %all-to-all-start.5 = ((bf16[16,24,16,128]{3,2,1,0:T(8,128)(2,1)}), bf16[16,24,16,128]{3,2,1,0:T(8,128)(2,1)S(1)}, u32[]{:S(2)}, u32[]{:S(2)}) async-start(bf16[16,24,16,128]{3,2,1,0:T(8,128)(2,1)} %bitcast.166), calls=%async_computation.5 | async-start | bytes 3145728 | tf_op jit(solution)/shard_map/all_to_all | solution.py:122
Sparse Core Ops, SparseCore 0:
  141.2 53.1 all-gather.7
  198.2 97.9 all-gather.5
where the time goes:
time: 375 us; the launch traced here: 374 us
  waiting for transfers between devices  232 us (62%)
  starting transfers between devices  38.3 us (10%)
  other arithmetic  28.7 us (8%)
  blocking collectives  21.6 us (6%)
  matrix products  21 us (6%)
  local copies, waits for them, and re-layouts  18.4 us (5%)
  between operations  14.3 us (4%)
    all_gather x2, waiting for transfers between devices, prefix_by_axis(): pieces = jax.tree.map(lambda part: lax.all_gather(part, axis), total)  90.7 us
    all_to_all x1, waiting for transfers between devices, body(): lax.all_to_all(owner_heads(*arrived), 'mem', split_axis=0, concat_axis=0,...  38.4 us
    all_to_all x1, waiting for transfers between devices, body(): lax.all_to_all(send_key, 'mem', split_axis=0, concat_axis=0, tiled=True)  36.4 us
    all_to_all x1, waiting for transfers between devices, body(): lax.all_to_all(send_value, 'mem', split_axis=0, concat_axis=0, tiled=True)  35.2 us
    all_to_all x1, waiting for transfers between devices, body(): lax.all_to_all(send_query, 'mem', split_axis=0, concat_axis=0, tiled=True)  24.1 us
    all_gather x1, blocking collectives, prefix_by_axis(): pieces = jax.tree.map(lambda part: lax.all_gather(part, axis), total)  14.4 us
    all_to_all x1, starting transfers between devices, body(): lax.all_to_all(send_rate, 'mem', split_axis=0, concat_axis=0, tiled=True)  10.1 us
    unnamed x28, local copies, waits for them, and re-layouts  9.28 us
  transfers between devices with their start and end apart: 8, of which 8 were waited for; matrix products, arithmetic and copies ran while one was open for 5% of the time, Pallas kernels for 0%

commit v1 on v0

v1 whole, which is shorter than its diff:
```python
import jax
import jax.numpy as jnp
from jax import lax
from jax.experimental import pallas as pl
from jax.experimental.pallas import tpu as pltpu
from jax.sharding import PartitionSpec as P

F32, BF16 = jnp.float32, jnp.bfloat16
TOK = 128
HD = 128
AUX = 16
PART_ROWS = 64
EPS = 1e-6
VMEM_LIMIT = 40 * 2**20


def iota(shape, dim):
    return lax.broadcasted_iota(jnp.int32, shape, dim)


def nt(a, b):
    return lax.dot_general(a, b, (((1,), (1,)), ((), ())), preferred_element_type=F32)


def tn(a, b):
    return lax.dot_general(a, b, (((0,), (0,)), ((), ())), preferred_element_type=F32)


def dot(a, b):
    return jnp.dot(a, b, preferred_element_type=F32)


def three_parts(x):
    hi = x.astype(BF16).astype(F32)
    mid = (x - hi).astype(BF16).astype(F32)
    return hi, mid, x - hi - mid


def pack_kernel(heads, q_ref, k_ref, v_ref, gamma_ref, ids_ref, weights_ref, out_ref):
    eye = (iota((TOK, TOK), 0) == iota((TOK, TOK), 1)).astype(BF16)
    gamma_rows = tn(gamma_ref[...], eye)
    ids = tn(ids_ref[...].astype(F32).astype(BF16), eye).astype(jnp.int32)
    w_hi, w_mid, w_lo = [tn(x.astype(BF16), eye) for x in three_parts(weights_ref[...])]
    memory = iota((heads, TOK), 0)
    hit0, hit1 = memory == ids[0:1], memory == ids[1:2]
    hits = jnp.where(hit0 | hit1, 1.0, 0.0).astype(BF16)
    earlier = (iota((TOK, TOK), 0) < iota((TOK, TOK), 1)).astype(BF16)
    before = dot(hits, earlier)
    rank0 = jnp.sum(jnp.where(hit0, before, 0.0), axis=0, keepdims=True)
    rank1 = jnp.sum(jnp.where(hit1, before, 0.0), axis=0, keepdims=True)
    row = iota((AUX, TOK), 0)
    shared = jnp.zeros((AUX, TOK), F32)
    entries = [ids[0:1].astype(F32), rank0, ids[1:2].astype(F32), rank1]
    for part in (w_hi, w_mid, w_lo):
        entries += [part[0:1], part[1:2]]
    for at, entry in enumerate(entries):
        shared = jnp.where(row == at + 1, entry, shared)
    for h in range(heads):
        lanes = slice(h * HD, (h + 1) * HD)
        out_ref[h, 0:TOK] = k_ref[:, lanes]
        out_ref[h, TOK : 2 * TOK] = v_ref[:, lanes]
        out_ref[h, 2 * TOK : 3 * TOK] = q_ref[:, lanes]
        aux = jnp.where(row == 0, gamma_rows[h : h + 1], shared)
        out_ref[h, 3 * TOK : 3 * TOK + AUX] = aux.astype(BF16)


def head_rates(rate_ref, head, scratch_ref):
    rates = rate_ref[...].astype(F32)
    mine = jnp.where(iota(rates.shape, 1) == head, rates, 0.0)
    scratch_ref[...] = jnp.broadcast_to(jnp.sum(mine, axis=1, keepdims=True), scratch_ref.shape)


def gather_kernel(memories, cap, in_ref, rate_ref, slots_ref, update_ref, rates_ref, after_ref):
    sources = in_ref.shape[0]
    slots = sources * cap
    head_rates(rate_ref, lax.axis_index("mem"), rates_ref)
    after_ref[...] = (iota((slots, slots), 1) > iota((slots, slots), 0)).astype(BF16)
    place = iota((memories * 2 * cap, TOK), 0)
    same = iota((TOK, TOK), 0) == iota((TOK, TOK), 1)
    ones = jnp.ones((TOK, HD), BF16)

    def gather(pair, carry):
        select, rows = [], []
        for side in range(2):
            source = 2 * pair + side
            aux = in_ref[source, 3 * TOK : 3 * TOK + AUX].astype(F32)
            at = aux[0:8].astype(jnp.int32)
            first = at[1:2] * (2 * cap) + at[2:3] + side * cap
            second = at[3:4] * (2 * cap) + at[4:5] + side * cap
            hit = (place == first) | (place == second)
            select.append(jnp.where(hit, 1.0, 0.0).astype(BF16))
            gamma = dot(jnp.where(same, aux[0:1], 0.0).astype(BF16), ones).astype(BF16)
            k = in_ref[source, 0:TOK]
            v = in_ref[source, TOK : 2 * TOK]
            q = in_ref[source, 2 * TOK : 3 * TOK]
            rows.append(jnp.concatenate([k, v, q, gamma], axis=1))
        got = dot(jnp.concatenate(select, axis=1), jnp.concatenate(rows, axis=0)).astype(BF16)
        at = pl.ds(pl.multiple_of(pair * 2 * cap, 2 * cap), 2 * cap)
        for m in range(memories):
            slots_ref[m, at, :] = got[m * 2 * cap : (m + 1) * 2 * cap]
        return carry

    lax.fori_loop(0, sources // 2, gather, 0)

    def update(m, carry):
        k = slots_ref[m, :, 0:HD].astype(F32)
        v = slots_ref[m, :, HD : 2 * HD]
        gamma = slots_ref[m, :, 3 * HD : 4 * HD]
        rate = rates_ref[pl.ds(m, 1), :]
        rest = dot(after_ref[...], gamma)
        kd = (k * jnp.exp(-rate * rest)).astype(BF16)
        added = tn(kd, v).astype(BF16)
        total = -rate * jnp.sum(gamma.astype(F32), axis=0, keepdims=True)
        row = iota((AUX, HD), 0)
        aux = jnp.zeros((AUX, HD), F32)
        for at, part in enumerate(three_parts(total)):
            aux = jnp.where(row == at, part, aux)
        for half in range(2):
            update_ref[2 * m + half, 0:PART_ROWS] = added[half * PART_ROWS : (half + 1) * PART_ROWS]
            update_ref[2 * m + half, PART_ROWS : PART_ROWS + AUX] = aux.astype(BF16)
        return carry

    lax.fori_loop(0, memories, update, 0)


def scan_kernel(in_ref, out_ref):
    state = jnp.zeros((PART_ROWS, HD), F32)
    for part in range(in_ref.shape[0]):
        out_ref[part] = state.astype(BF16)
        aux = in_ref[part, PART_ROWS : PART_ROWS + AUX].astype(F32)
        fade = jnp.exp(aux[0:1] + aux[1:2] + aux[2:3])
        state = fade * state + in_ref[part, 0:PART_ROWS].astype(F32)


def intra_kernel(slots_ref, rate_ref, raw_ref, fade_ref, rates_ref, upto_ref):
    memories, slots, _ = slots_ref.shape
    head_rates(rate_ref, lax.axis_index("mem"), rates_ref)
    causal = iota((slots, slots), 0) >= iota((slots, slots), 1)
    upto_ref[...] = causal.astype(BF16)

    def one(m, carry):
        k = slots_ref[m, :, 0:HD]
        v = slots_ref[m, :, HD : 2 * HD]
        q = slots_ref[m, :, 2 * HD : 3 * HD]
        gamma = slots_ref[m, :, 3 * HD : 4 * HD]
        rate = rates_ref[pl.ds(m, 1), :]
        wide = jnp.concatenate([gamma] * (slots // HD), axis=1).astype(F32)
        later = iota((slots, slots), 0) > iota((slots, slots), 1)
        spread = dot(upto_ref[...], jnp.where(later, wide, 0.0).astype(BF16))
        fade_ref[m] = jnp.exp(-rate * dot(upto_ref[...], gamma))
        wide_rate = jnp.concatenate([rate] * (slots // HD), axis=1)
        decay = jnp.exp(-wide_rate * spread)
        keep = iota((slots, slots), 0) >= iota((slots, slots), 1)
        weights = jnp.where(keep, decay * nt(q, k), 0.0).astype(BF16)
        raw_ref[m] = dot(weights, v)
        return carry

    lax.fori_loop(0, memories, one, 0)


def finish_kernel(cap, in_ref, slots_ref, raw_ref, fade_ref, state_ref, gain_ref, out_ref, made_ref):
    memories, slots, _ = slots_ref.shape
    sources = in_ref.shape[0]

    def one(m, carry):
        q = slots_ref[m, :, 2 * HD : 3 * HD]
        raw = raw_ref[m] + fade_ref[m] * dot(q, state_ref[m])
        mean = jnp.mean(raw * raw, axis=1, keepdims=True)
        made_ref[m] = (raw * lax.rsqrt(mean + EPS)).astype(BF16)
        return carry

    lax.fori_loop(0, memories, one, 0)
    gain = gain_ref[pl.ds(lax.axis_index("mem"), 1), :]
    width = memories * 2 * cap
    place = iota((TOK, width), 1)
    eye = (iota((TOK, TOK), 0) == iota((TOK, TOK), 1)).astype(BF16)

    def mix(pair, carry):
        at = pl.ds(pl.multiple_of(pair * 2 * cap, 2 * cap), 2 * cap)
        rows = jnp.concatenate([made_ref[m, at, :] for m in range(memories)], axis=0)
        for side in range(2):
            source = 2 * pair + side
            aux = nt(eye, in_ref[source, 3 * TOK : 3 * TOK + AUX])
            number = aux.astype(jnp.int32)
            first = number[:, 1:2] * (2 * cap) + number[:, 2:3] + side * cap
            second = number[:, 3:4] * (2 * cap) + number[:, 4:5] + side * cap
            w0 = aux[:, 5:6] + aux[:, 7:8] + aux[:, 9:10]
            w1 = aux[:, 6:7] + aux[:, 8:9] + aux[:, 10:11]
            pick0 = jnp.where(place == first, 1.0, 0.0).astype(BF16)
            pick1 = jnp.where(place == second, 1.0, 0.0).astype(BF16)
            mixed = w0 * dot(pick0, rows) + w1 * dot(pick1, rows)
            out_ref[source] = (gain * mixed).astype(BF16)
        return carry

    lax.fori_loop(0, sources // 2, mix, 0)


def unpack_kernel(in_ref, out_ref):
    for h in range(in_ref.shape[0]):
        out_ref[:, h * HD : (h + 1) * HD] = in_ref[h]


def call(kernel, outs, scratch=(), flops=0, moved=0, exps=0):
    return pl.pallas_call(
        kernel,
        out_shape=outs,
        scratch_shapes=list(scratch),
        compiler_params=pltpu.CompilerParams(vmem_limit_bytes=VMEM_LIMIT),
        cost_estimate=pl.CostEstimate(flops=flops, bytes_accessed=moved, transcendentals=exps),
    )


def body(queries, keys, values, gamma, rate, route_ids, route_weights, norm_gain):
    heads = gamma.shape[1]
    memories = rate.shape[0]
    sources = lax.axis_size("mem")
    parts = lax.axis_size("seq")
    cap = 3 * TOK // memories
    slots = sources * cap
    like = jax.ShapeDtypeStruct

    send = call(
        lambda *refs: pack_kernel(heads, *refs),
        like((heads, 3 * TOK + AUX, HD), BF16),
    )(queries, keys, values, gamma, route_ids, route_weights)
    arrived = lax.all_to_all(send, "mem", 0, 0, tiled=True)

    rates = pltpu.VMEM((memories, HD), F32)
    square = pltpu.VMEM((slots, slots), BF16)
    slot_rows, update = call(
        lambda *refs: gather_kernel(memories, cap, *refs),
        (
            like((memories, slots, 4 * HD), BF16),
            like((parts, PART_ROWS + AUX, HD), BF16),
        ),
        (rates, square),
    )(arrived, rate)
    pieces = lax.all_to_all(update, "seq", 0, 0, tiled=True)
    raw, fade = call(
        intra_kernel,
        (like((memories, slots, HD), F32), like((memories, slots, HD), F32)),
        (rates, square),
        flops=memories * slots * slots * HD * 10,
        moved=memories * slots * HD * 16,
        exps=memories * slots * slots,
    )(slot_rows, rate)
    before = call(scan_kernel, like((parts, PART_ROWS, HD), BF16))(pieces)
    state = lax.all_to_all(before, "seq", 0, 0, tiled=True).reshape(memories, HD, HD)
    mixed = call(
        lambda *refs: finish_kernel(cap, *refs),
        like((sources, TOK, HD), BF16),
        (pltpu.VMEM((memories, slots, HD), BF16),),
    )(arrived, slot_rows, raw, fade, state, norm_gain.reshape(heads, HD))
    returned = lax.all_to_all(mixed, "mem", 0, 0, tiled=True)
    return call(unpack_kernel, like((TOK, heads * HD), BF16))(returned)


def solution(mesh):
    split = P(("seq", "mem"), None)
    return jax.shard_map(
        body,
        mesh=mesh,
        in_specs=(split, split, split, split, P(), split, split, P()),
        out_specs=split,
        check_vma=False,
    )
```

time: 375 us -> 166 us (0.44)
  waiting for transfers between devices: 232 us -> 0.01 us
  blocking collectives: 21.6 us -> 104 us
  Pallas kernels: 0 us -> 38.3 us
  starting transfers between devices: 38.3 us -> 5.42 us
  other arithmetic: 28.7 us -> 0 us
  matrix products: 21 us -> 0 us
  between operations: 14.3 us -> 0.08 us
    all_to_all x6 -> x1, waiting for transfers between devices: 142 us -> 0.01 us  [body(): lax.all_to_all(before, 'seq', 0, 0, tiled=True).reshape(memories, HD, HD)]
    all_to_all x0 -> x3, blocking collectives: none -> 104 us  [the longest x1 50.9 us: body(): arrived = lax.all_to_all(send, 'mem', 0, 0, tiled=True)]
    all_gather x2 -> x0, waiting for transfers between devices: 90.7 us -> none  [prefix_by_axis(): pieces = jax.tree.map(lambda part: lax.all_gather(part, axis), total)]
    pallas_call x0 -> x6, Pallas kernels: none -> 38.3 us  [the longest x1 14.9 us: body(): call(lambda *refs: finish_kernel(cap, *refs), like((sources, TOK, HD), BF...]
    all_to_all x6 -> x1, starting transfers between devices: 38.2 us -> 5.42 us  [body(): lax.all_to_all(before, 'seq', 0, 0, tiled=True).reshape(memories, HD, HD)]
    dot_general x9 -> x0, matrix products: 21 us -> none  [the longest x1 6.83 us: owner_heads(): jnp.einsum('btsh,bshe->bthe', weights, value_rows, preferred_element_type...]
    all_gather x1 -> x0, blocking collectives: 14.4 us -> none  [prefix_by_axis(): pieces = jax.tree.map(lambda part: lax.all_gather(part, axis), total)]
    mul x8 -> x0, other arithmetic: 11.5 us -> none  [the longest x1 6.04 us: owner_heads(): states = entering[1] + entering[0][:, :, None, None] * before_state[None]]
  transfers between devices with their start and end apart: 8 -> 1, of which waited for: 8 -> 0; matrix products, arithmetic and copies ran while one was open for 5% -> 0% of each run, Pallas kernels for 0% -> 6%
where the time goes in v1:
time: 166 us
  blocking collectives  104 us (63%)
  Pallas kernels  38.3 us (23%)
  local copies, waits for them, and re-layouts  18.1 us (11%)
  starting transfers between devices  5.42 us (3%)
    all_to_all x1, blocking collectives, body(): arrived = lax.all_to_all(send, 'mem', 0, 0, tiled=True)  50.9 us
    all_to_all x1, blocking collectives, body(): pieces = lax.all_to_all(update, 'seq', 0, 0, tiled=True)  30.6 us
    all_to_all x1, blocking collectives, body(): returned = lax.all_to_all(mixed, 'mem', 0, 0, tiled=True)  22.4 us
    unnamed x25, local copies, waits for them, and re-layouts  18.1 us
    pallas_call x1, Pallas kernels, body(): call(lambda *refs: finish_kernel(cap, *refs), like((sources, TOK, HD), BF...  14.9 us
    pallas_call x1, Pallas kernels, body(): call(lambda *refs: gather_kernel(memories, cap, *refs), (like((memories,...  11.2 us
    pallas_call x1, Pallas kernels, body(): call(intra_kernel, (like((memories, slots, HD), F32), like((memories, slo...  9.99 us
    all_to_all x1, starting transfers between devices, body(): lax.all_to_all(before, 'seq', 0, 0, tiled=True).reshape(memories, HD, HD)  5.42 us
  transfers between devices with their start and end apart: 1, of which 0 were waited for; matrix products, arithmetic and copies ran while one was open for 0% of the time, Pallas kernels for 6%

profile of v1, /device:TPU:1, one launch (start us, length us, event | category | flops | bytes accessed | tf_op | source)
XLA Modules:
  0.0 165.8 jit_solution(7643328923423140979)
XLA Ops:
  0.0 0.8 copy.9.refs_3_
  0.8 0.8 copy.10.refs_4_
  1.6 0.8 copy.11.refs_5_
  2.4 0.0 copy-start.6
  2.4 1.0 copy-done.6
  3.4 0.0 copy-start.7
  3.4 1.0 copy-done.7
  4.5 0.0 copy-start.8
  4.5 1.0 copy-done.8
  5.5 0.0 copy-start.10
  5.5 0.4 shard_map.82
  5.9 50.9 %all_to_all.20.refs_0_ = bf16[16,400,128]{2,1,0:T(8,128)(2,1)S(1)} all-to-all(bf16[16,400,128]{2,1,0:T(8,128)(2,1)S(1)} %shard_map.82), channel_id=1, replica_groups=mesh['seq'=32,'mem'=16] {'mem'}, dimensions={0} | all-to-all | bytes 3276800 | tf_op jit(solution)/shard_map/all_to_all | solution.py:226
  56.8 0.0 copy-done.10
  56.8 11.2 %shard_map.83 = (bf16[16,384,512]{2,1,0:T(8,128)(2,1)S(1)}, bf16[32,80,128]{2,1,0:T(8,128)(2,1)S(1)}) custom-call(bf16[16,400,128]{2,1,0:T(8,128)(2,1)S(1)} %all_to_all.20.refs_0_, bf16[16,16]{1,0:T(8,128)(2,1)S(1)} %copy-done.10), custom_call_target="tpu_custom_call" | custom-call | tf_op jit(solution)/shard_map/pallas_call | solution.py:230
  68.0 0.0 copy-start
  68.0 2.6 %copy-done = bf16[16,384,512]{2,1,0:T(8,128)(2,1)} copy-done((bf16[16,384,512]{2,1,0:T(8,128)(2,1)}, bf16[16,384,512]{2,1,0:T(8,128)(2,1)S(1)}, u32[]{:S(2)}) %copy-start) | copy-done | bytes 6291480
  70.6 30.6 %all_to_all.21.in_ref = bf16[32,80,128]{2,1,0:T(8,128)(2,1)S(1)} all-to-all(bf16[32,80,128]{2,1,0:T(8,128)(2,1)S(1)} %get-tuple-element.12), channel_id=1, replica_groups=mesh['seq'=32,'mem'=16] {'seq'}, dimensions={0} | all-to-all | bytes 1310720 | tf_op jit(solution)/shard_map/all_to_all | solution.py:238
  101.3 0.9 shard_map.85
  102.2 5.4 %all-to-all-start.2 = ((bf16[32,64,128]{2,1,0:T(8,128)(2,1)}), bf16[32,64,128]{2,1,0:T(8,128)(2,1)S(1)}, u32[]{:S(2)}, u32[]{:S(2)}) async-start(bf16[32,64,128]{2,1,0:T(8,128)(2,1)} %shard_map.85), calls=%async_computation.2 | async-start | bytes 1048576 | tf_op jit(solution)/shard_map/all_to_all | solution.py:248
  107.6 0.0 copy-start.1
  107.7 2.8 %copy-done.1 = bf16[16,384,512]{2,1,0:T(8,128)(2,1)S(1)} copy-done((bf16[16,384,512]{2,1,0:T(8,128)(2,1)S(1)}, bf16[16,384,512]{2,1,0:T(8,128)(2,1)}, u32[]{:S(2)}) %copy-start.1) | copy-done | bytes 6291480
  110.4 0.0 copy-start.9
  110.4 10.0 %shard_map.84 = (f32[16,384,128]{2,1,0:T(8,128)S(1)}, f32[16,384,128]{2,1,0:T(8,128)S(1)}) custom-call(bf16[16,384,512]{2,1,0:T(8,128)(2,1)S(1)} %copy-done.1, bf16[16,16]{1,0:T(8,128)(2,1)S(1)} %copy-done.10), custom_call_target="tpu_custom_call" | custom-call | flops 3019898880 | bytes 12582912 | tf_op jit(solution)/shard_map/pallas_call | solution.py:239
  120.4 0.0 copy-start.2
  120.4 1.7 %copy-done.2 = f32[16,384,128]{2,1,0:T(8,128)} copy-done((f32[16,384,128]{2,1,0:T(8,128)}, f32[16,384,128]{2,1,0:T(8,128)S(1)}, u32[]{:S(2)}) %copy-start.2) | copy-done | bytes 3145752
  122.1 0.0 copy-start.4
  122.1 1.6 copy-done.4
  123.8 0.0 all-to-all-done.2
  123.8 0.0 copy-done.9
  123.8 0.0 copy-start.3
  123.8 1.9 %copy-done.3 = f32[16,384,128]{2,1,0:T(8,128)S(1)} copy-done((f32[16,384,128]{2,1,0:T(8,128)S(1)}, f32[16,384,128]{2,1,0:T(8,128)}, u32[]{:S(2)}) %copy-start.3) | copy-done | bytes 3145752
  125.7 0.0 copy-start.5
  125.7 1.9 %copy-done.5 = f32[16,384,128]{2,1,0:T(8,128)S(1)} copy-done((f32[16,384,128]{2,1,0:T(8,128)S(1)}, f32[16,384,128]{2,1,0:T(8,128)}, u32[]{:S(2)}) %copy-start.5) | copy-done | bytes 3145752
  127.6 14.9 %shard_map.86 = bf16[16,128,128]{2,1,0:T(8,128)(2,1)S(1)} custom-call(bf16[16,400,128]{2,1,0:T(8,128)(2,1)S(1)} %all_to_all.20.refs_0_, bf16[16,384,512]{2,1,0:T(8,128)(2,1)} %copy-done, f32[16,384,128]{2,1,0:T(8,128)S(1)} %copy-done.3, f32[16,384,128]{2,1,0:T(8,128)S(1)} %copy-done.5, bf16[16,128,128]{2,1,0:T(8,128)(2,1)S(1)} %bitcast.2, f32[16,128]{1,0:T(8,128)S(1)} %bitcast.3), custom_call_target="tpu_custom_call" | custom-call | tf_op jit(solution)/shard_map/pallas_call | solution.py:249
  142.5 22.4 %all_to_all.22.in_ref = bf16[16,128,128]{2,1,0:T(8,128)(2,1)S(1)} all-to-all(bf16[16,128,128]{2,1,0:T(8,128)(2,1)S(1)} %shard_map.86), channel_id=1, replica_groups=mesh['seq'=32,'mem'=16] {'mem'}, dimensions={0} | all-to-all | bytes 1048576 | tf_op jit(solution)/shard_map/all_to_all | solution.py:254
  164.9 0.9 shard_map.87
Async XLA Ops:
  2.4 1.0 copy-start.6
  3.4 1.0 copy-start.7
  4.5 1.0 copy-start.8
  5.5 51.3 %copy-start.10 = (bf16[16,16]{1,0:T(8,128)(2,1)S(1)}, bf16[16,16]{1,0:T(8,128)(2,1)}, u32[]{:S(2)}) copy-start(bf16[16,16]{1,0:T(8,128)(2,1)} %rate_ref.1) | copy-start | bytes 1540
  68.0 2.6 %copy-start = (bf16[16,384,512]{2,1,0:T(8,128)(2,1)}, bf16[16,384,512]{2,1,0:T(8,128)(2,1)S(1)}, u32[]{:S(2)}) copy-start(bf16[16,384,512]{2,1,0:T(8,128)(2,1)S(1)} %get-tuple-element.9.slots_ref.refs_1_) | copy-start | bytes 18874372
  102.2 21.6 %all-to-all-start.2 = ((bf16[32,64,128]{2,1,0:T(8,128)(2,1)}), bf16[32,64,128]{2,1,0:T(8,128)(2,1)S(1)}, u32[]{:S(2)}, u32[]{:S(2)}) async-start(bf16[32,64,128]{2,1,0:T(8,128)(2,1)} %shard_map.85), calls=%async_computation.2 | async-start | bytes 1048576 | tf_op jit(solution)/shard_map/all_to_all | solution.py:248
  107.6 2.8 %copy-start.1 = (bf16[16,384,512]{2,1,0:T(8,128)(2,1)S(1)}, bf16[16,384,512]{2,1,0:T(8,128)(2,1)}, u32[]{:S(2)}) copy-start(bf16[16,384,512]{2,1,0:T(8,128)(2,1)} %copy-done) | copy-start | bytes 18874372
  110.4 13.4 %copy-start.9 = (f32[2048]{0:T(1024)S(1)}, f32[2048]{0:T(1024)}, u32[]{:S(2)}) copy-start(f32[2048]{0:T(1024)} %param.15) | copy-start | bytes 24580
  120.4 1.7 %copy-start.2 = (f32[16,384,128]{2,1,0:T(8,128)}, f32[16,384,128]{2,1,0:T(8,128)S(1)}, u32[]{:S(2)}) copy-start(f32[16,384,128]{2,1,0:T(8,128)S(1)} %get-tuple-element.10.refs_2_) | copy-start | bytes 9437188
  122.1 1.7 copy-start.4
  123.8 1.9 %copy-start.3 = (f32[16,384,128]{2,1,0:T(8,128)S(1)}, f32[16,384,128]{2,1,0:T(8,128)}, u32[]{:S(2)}) copy-start(f32[16,384,128]{2,1,0:T(8,128)} %copy-done.2) | copy-start | bytes 9437188
  125.7 1.9 %copy-start.5 = (f32[16,384,128]{2,1,0:T(8,128)S(1)}, f32[16,384,128]{2,1,0:T(8,128)}, u32[]{:S(2)}) copy-start(f32[16,384,128]{2,1,0:T(8,128)} %copy-done.4) | copy-start | bytes 9437188

commit v2 on v1

v2 whole, which is shorter than its diff:
```python
import jax
import jax.numpy as jnp
from jax import lax
from jax.experimental import pallas as pl
from jax.experimental.pallas import tpu as pltpu
from jax.sharding import PartitionSpec as P

F32, BF16 = jnp.float32, jnp.bfloat16
TOK = 128
HD = 128
AUX = 16
KV = 2 * TOK + AUX
PART_ROWS = 64
EPS = 1e-6
VMEM_ALL = 58_000_000


def iota(shape, dim):
    return lax.broadcasted_iota(jnp.int32, shape, dim)


def nt(a, b):
    return lax.dot_general(a, b, (((1,), (1,)), ((), ())), preferred_element_type=F32)


def tn(a, b):
    return lax.dot_general(a, b, (((0,), (0,)), ((), ())), preferred_element_type=F32)


def dot(a, b):
    return jnp.dot(a, b, preferred_element_type=F32)


def three_parts(x):
    hi = x.astype(BF16).astype(F32)
    mid = (x - hi).astype(BF16).astype(F32)
    return hi, mid, x - hi - mid


def own_head():
    return lax.axis_index("mem")


def pack_kernel(
    heads, q_ref, k_ref, v_ref, gamma_ref, ids_ref, weights_ref, out_ref, sem
):
    copies = []
    for h in range(heads):
        for at, ref in ((0, k_ref), (TOK, v_ref), (KV, q_ref)):
            copies.append(
                pltpu.make_async_copy(
                    ref.at[:, h * HD : (h + 1) * HD],
                    out_ref.at[h, at : at + TOK],
                    sem.at[len(copies)],
                )
            )
    for copy in copies:
        copy.start()
    ids = ids_ref[...]
    w_hi, w_mid, w_lo = three_parts(weights_ref[...])
    memory = iota((heads, TOK), 0)
    hit0, hit1 = memory == ids[0:1], memory == ids[1:2]
    hits = jnp.where(hit0 | hit1, 1.0, 0.0).astype(BF16)
    earlier = (iota((TOK, TOK), 0) < iota((TOK, TOK), 1)).astype(BF16)
    before = dot(hits, earlier)
    rank0 = jnp.sum(jnp.where(hit0, before, 0.0), axis=0, keepdims=True)
    rank1 = jnp.sum(jnp.where(hit1, before, 0.0), axis=0, keepdims=True)
    row = iota((AUX, TOK), 0)
    shared = jnp.zeros((AUX, TOK), F32)
    entries = [ids[0:1].astype(F32), rank0, ids[1:2].astype(F32), rank1]
    for part in (w_hi, w_mid, w_lo):
        entries += [part[0:1], part[1:2]]
    for at, entry in enumerate(entries):
        shared = jnp.where(row == at + 1, entry, shared)
    gamma_rows = gamma_ref[...].astype(F32)
    for h in range(heads):
        aux = jnp.where(row == 0, gamma_rows[h : h + 1], shared)
        out_ref[h, 2 * TOK : KV] = aux.astype(BF16)
    for copy in copies:
        copy.wait()


def head_rates(rate_ref, head, scratch_ref):
    rates = rate_ref[...].astype(F32)
    mine = jnp.where(iota(rates.shape, 1) == head, rates, 0.0)
    scratch_ref[...] = jnp.broadcast_to(jnp.sum(mine, axis=1, keepdims=True), scratch_ref.shape)


def slot_ids(aux, cap, side):
    at = aux[0:8].astype(jnp.int32)
    first = at[1:2] * (2 * cap) + at[2:3] + side * cap
    second = at[3:4] * (2 * cap) + at[4:5] + side * cap
    return first, second


def gather_kernel(
    cap, in_ref, rate_ref, slots_out, update_ref, rows_ref, slots_ref, rest_ref, rates_ref, later_ref, sem, slots_sem
):
    sources = in_ref.shape[0]
    memories, slots, _ = slots_ref.shape
    width = memories * 2 * cap

    def arriving(source):
        return pltpu.make_async_copy(in_ref.at[source, 0:KV], rows_ref.at[source], sem.at[source])

    for source in range(sources):
        arriving(source).start()
    head_rates(rate_ref, own_head(), rates_ref)
    after = (iota((TOK, TOK), 0) > iota((TOK, TOK), 1)).astype(BF16)
    memory = iota((memories, TOK), 0)
    for source in range(sources):
        arriving(source).wait()

    hits, gammas = [], []
    for source in range(sources):
        aux = rows_ref[source, 2 * TOK : KV].astype(F32)
        at = aux.astype(jnp.int32)
        hit = (memory == at[1:2]) | (memory == at[3:4])
        gammas.append(jnp.where(hit, aux[0:1], 0.0))
    inside = dot(jnp.concatenate(gammas, axis=0).astype(BF16), after)
    behind = jnp.zeros((memories, 1), F32)
    for source in reversed(range(sources)):
        own = inside[source * memories : (source + 1) * memories]
        later_ref[source] = own + behind
        behind = behind + own[:, 0:1] + gammas[source][:, 0:1]
    total = -rates_ref[...] * behind

    place = iota((width, TOK), 0)

    def gather(pair, carry):
        rows, select, rest = [], [], jnp.zeros((width, TOK), F32)
        for side in range(2):
            source = 2 * pair + side
            aux = rows_ref[source, 2 * TOK : KV].astype(F32)
            at = aux.astype(jnp.int32)
            later = later_ref[source]
            rest0 = jnp.sum(jnp.where(memory == at[1:2], later, 0.0), axis=0, keepdims=True)
            rest1 = jnp.sum(jnp.where(memory == at[3:4], later, 0.0), axis=0, keepdims=True)
            first, second = slot_ids(aux, cap, side)
            hit0, hit1 = place == first, place == second
            select.append(jnp.where(hit0 | hit1, 1.0, 0.0).astype(BF16))
            rest = rest + jnp.where(hit0, rest0, jnp.where(hit1, rest1, 0.0))
            rows.append(
                jnp.concatenate([rows_ref[source, 0:TOK], rows_ref[source, TOK : 2 * TOK]], axis=1)
            )
        rest = jnp.broadcast_to(jnp.sum(rest, axis=1, keepdims=True), (width, HD))
        got = dot(jnp.concatenate(select, axis=1), jnp.concatenate(rows, axis=0)).astype(BF16)
        at = pl.ds(pl.multiple_of(pair * 2 * cap, 2 * cap), 2 * cap)
        for m in range(memories):
            slots_ref[m, at, :] = got[m * 2 * cap : (m + 1) * 2 * cap]
            rest_ref[m, at, :] = rest[m * 2 * cap : (m + 1) * 2 * cap]
        leaving(pair).start()
        return carry

    def leaving(pair):
        at = pl.ds(pl.multiple_of(pair * 2 * cap, 2 * cap), 2 * cap)
        return pltpu.make_async_copy(slots_ref.at[:, at], slots_out.at[:, at], slots_sem.at[pair])

    lax.fori_loop(0, sources // 2, gather, 0)

    def update(m, carry):
        k = slots_ref[m, :, 0:HD].astype(F32)
        v = slots_ref[m, :, HD : 2 * HD]
        kd = (k * jnp.exp(-rates_ref[pl.ds(m, 1), :] * rest_ref[m])).astype(BF16)
        added = tn(kd, v).astype(BF16)
        for half in range(2):
            part = added[half * PART_ROWS : (half + 1) * PART_ROWS]
            update_ref[2 * m + half, 0:PART_ROWS] = part
        return carry

    lax.fori_loop(0, memories, update, 0, unroll=2)
    row = iota((AUX, HD), 0)
    for m in range(memories):
        aux = jnp.zeros((AUX, HD), F32)
        for at, part in enumerate(three_parts(total[m : m + 1])):
            aux = jnp.where(row == at, part, aux)
        for half in range(2):
            update_ref[2 * m + half, PART_ROWS : PART_ROWS + AUX] = aux.astype(BF16)
    for pair in range(sources // 2):
        leaving(pair).wait()


def scan_kernel(in_ref, out_ref):
    state = jnp.zeros((PART_ROWS, HD), F32)
    for part in range(in_ref.shape[0]):
        out_ref[part] = state.astype(BF16)
        aux = in_ref[part, PART_ROWS : PART_ROWS + AUX].astype(F32)
        fade = jnp.exp(aux[0:1] + aux[1:2] + aux[2:3])
        state = fade * state + in_ref[part, 0:PART_ROWS].astype(F32)


def route_kernel(cap, in_ref, slots_ref, pick_ref):
    memories = slots_ref.shape[0]
    width = memories * 2 * cap
    eye = iota((TOK, TOK), 0) == iota((TOK, TOK), 1)
    ones = jnp.ones((TOK, HD), BF16)
    place = iota((width, TOK), 0)
    rows, select = [], []
    for side in range(2):
        aux = in_ref[side, 2 * TOK : KV].astype(F32)
        gamma = dot(jnp.where(eye, aux[0:1], 0.0).astype(BF16), ones).astype(BF16)
        rows.append(jnp.concatenate([in_ref[side, KV : KV + TOK], gamma], axis=1))
        first, second = slot_ids(aux, cap, side)
        hit = (place == first) | (place == second)
        select.append(jnp.where(hit, 1.0, 0.0).astype(BF16))
    got = dot(jnp.concatenate(select, axis=1), jnp.concatenate(rows, axis=0)).astype(BF16)
    for m in range(memories):
        slots_ref[m] = got[m * 2 * cap : (m + 1) * 2 * cap]
    place = iota((TOK, width), 1)
    for side in range(2):
        aux = nt(eye.astype(BF16), in_ref[side, 2 * TOK : KV])
        at = aux.astype(jnp.int32)
        first = at[:, 1:2] * (2 * cap) + at[:, 2:3] + side * cap
        second = at[:, 3:4] * (2 * cap) + at[:, 4:5] + side * cap
        w0 = aux[:, 5:6] + aux[:, 7:8] + aux[:, 9:10]
        w1 = aux[:, 6:7] + aux[:, 8:9] + aux[:, 10:11]
        pick = jnp.where(place == first, w0, jnp.where(place == second, w1, 0.0))
        pick_ref[0, side * TOK : (side + 1) * TOK] = pick.astype(BF16)


def intra_kernel(kv_ref, qg_ref, rate_ref, raw_ref, faded_ref, rates_ref, sums_ref):
    slots = kv_ref.shape[1]
    m = pl.program_id(0)
    tri = iota((TOK, TOK), 0) - iota((TOK, TOK), 1)

    @pl.when(m == 0)
    def _():
        head_rates(rate_ref, own_head(), rates_ref)
        sums_ref[0:TOK] = (tri >= 0).astype(BF16)
        sums_ref[TOK : 2 * TOK] = (tri < 0).astype(BF16)

    rate = rates_ref[pl.ds(m, 1), :]
    behind = []
    faded_all = jnp.ones((1, HD), F32)
    for b in range(slots // TOK):
        at = slice(b * TOK, (b + 1) * TOK)
        q = qg_ref[0, at, 0:HD]
        gamma = qg_ref[0, at, HD : 2 * HD]
        masked = jnp.where(tri > 0, gamma.astype(F32), 0.0).astype(BF16)
        sums = dot(sums_ref[...], jnp.concatenate([masked, gamma], axis=1))
        inside = jnp.where(tri >= 0, jnp.exp(-rate * sums[0:TOK, 0:TOK]), 0.0)
        fade = jnp.exp(-rate * sums[0:TOK, TOK : 2 * TOK])
        faded_ref[0, at] = (q.astype(F32) * (fade * faded_all)).astype(BF16)
        decay = jnp.concatenate([fade * row for row in behind] + [inside], axis=1)
        scores = nt(q, kv_ref[0, 0 : (b + 1) * TOK, 0:HD])
        weights = (decay * scores).astype(BF16)
        raw_ref[0, at] = dot(weights, kv_ref[0, 0 : (b + 1) * TOK, HD : 2 * HD])
        whole = fade[TOK - 1 : TOK]
        faded_all = faded_all * whole
        rest = jnp.exp(-rate * sums[TOK : 2 * TOK, TOK : 2 * TOK])
        behind = [row * whole for row in behind] + [rest.T]


def finish_kernel(
    cap, faded_hbm, raw_hbm, pick_hbm, state_ref, gain_ref, out_ref, faded_ref, raw_ref, pick_ref, made_ref, sems, pick_sem
):
    memories = faded_ref.shape[0]
    pairs = pick_ref.shape[0]

    def arriving(m):
        return (
            pltpu.make_async_copy(faded_hbm.at[m], faded_ref.at[m], sems.at[0, m]),
            pltpu.make_async_copy(raw_hbm.at[m], raw_ref.at[m], sems.at[1, m]),
        )

    picks = pltpu.make_async_copy(pick_hbm, pick_ref, pick_sem)
    for m in range(memories):
        for copy in arriving(m):
            copy.start()
    picks.start()

    def one(m, carry):
        for copy in arriving(m):
            copy.wait()
        raw = raw_ref[m] + dot(faded_ref[m], state_ref[m])
        mean = jnp.mean(raw * raw, axis=1, keepdims=True)
        made_ref[m] = (raw * lax.rsqrt(mean + EPS)).astype(BF16)
        return carry

    lax.fori_loop(0, memories, one, 0, unroll=2)
    picks.wait()
    gain = gain_ref[pl.ds(own_head(), 1), :]

    def mix(pair, carry):
        at = pl.ds(pl.multiple_of(pair * 2 * cap, 2 * cap), 2 * cap)
        rows = jnp.concatenate([made_ref[m, at, :] for m in range(memories)], axis=0)
        mixed = (gain * dot(pick_ref[pair], rows)).astype(BF16)
        for side in range(2):
            out_ref[2 * pair + side] = mixed[side * TOK : (side + 1) * TOK]
        return carry

    lax.fori_loop(0, pairs, mix, 0, unroll=2)


def unpack_kernel(in_ref, out_ref):
    for h in range(in_ref.shape[0]):
        out_ref[:, h * HD : (h + 1) * HD] = in_ref[h]


like = jax.ShapeDtypeStruct
ANY = pl.BlockSpec(memory_space=pl.ANY)
WHOLE = pl.BlockSpec(memory_space=pltpu.VMEM)
DMA = pltpu.SemaphoreType.DMA


def call(kernel, outs, ins, out_specs, room, scratch=(), grid=(), flops=0, moved=0):
    return pl.pallas_call(
        kernel,
        out_shape=outs,
        grid=grid,
        in_specs=ins,
        out_specs=out_specs,
        scratch_shapes=list(scratch),
        compiler_params=pltpu.CompilerParams(vmem_limit_bytes=VMEM_ALL - room),
        cost_estimate=pl.CostEstimate(flops=flops, bytes_accessed=moved, transcendentals=0),
    )


def pack(heads):
    return call(
        lambda *refs: pack_kernel(heads, *refs),
        like((heads, KV + TOK, HD), BF16),
        [ANY, ANY, ANY, WHOLE, WHOLE, WHOLE],
        WHOLE,
        -2_000_000,
        (DMA((3 * heads,)),),
    )


def gather(memories, sources, parts):
    cap = 3 * TOK // memories
    slots = sources * cap
    return call(
        lambda *refs: gather_kernel(cap, *refs),
        (
            like((memories, slots, 2 * HD), BF16),
            like((parts, PART_ROWS + AUX, HD), BF16),
        ),
        [ANY, WHOLE],
        (ANY, WHOLE),
        2_500_000,
        (
            pltpu.VMEM((sources, KV, HD), BF16),
            pltpu.VMEM((memories, slots, 2 * HD), BF16),
            pltpu.VMEM((memories, slots, HD), F32),
            pltpu.VMEM((memories, HD), F32),
            pltpu.VMEM((sources, memories, TOK), F32),
            DMA((sources,)),
            DMA((sources // 2,)),
        ),
    )


def scan(parts):
    return call(scan_kernel, like((parts, PART_ROWS, HD), BF16), [WHOLE], WHOLE, 40_000_000)


def route(memories, sources):
    cap = 3 * TOK // memories
    slots = sources * cap
    pairs = sources // 2
    width = memories * 2 * cap
    return call(
        lambda *refs: route_kernel(cap, *refs),
        (like((memories, slots, 2 * HD), BF16), like((pairs, 2 * TOK, width), BF16)),
        [pl.BlockSpec((2, KV + TOK, HD), lambda p: (p, 0, 0))],
        (
            pl.BlockSpec((memories, 2 * cap, 2 * HD), lambda p: (0, p, 0)),
            pl.BlockSpec((1, 2 * TOK, width), lambda p: (p, 0, 0)),
        ),
        1_000_000,
        grid=(pairs,),
        flops=10**10,
        moved=8 * 2**20,
    )


def intra(memories, sources):
    slots = sources * (3 * TOK // memories)
    one = pl.BlockSpec((1, slots, HD), lambda m: (m, 0, 0))
    two = pl.BlockSpec((1, slots, 2 * HD), lambda m: (m, 0, 0))
    return call(
        intra_kernel,
        (like((memories, slots, HD), F32), like((memories, slots, HD), BF16)),
        [two, two, WHOLE],
        (one, one),
        1_000_000,
        (pltpu.VMEM((memories, HD), F32), pltpu.VMEM((2 * TOK, TOK), BF16)),
        grid=(memories,),
        flops=10**10,
        moved=10 * 2**20,
    )


def finish(memories, sources):
    cap = 3 * TOK // memories
    slots = sources * cap
    pairs = sources // 2
    return call(
        lambda *refs: finish_kernel(cap, *refs),
        like((sources, TOK, HD), BF16),
        [ANY, ANY, ANY, WHOLE, WHOLE],
        WHOLE,
        1_300_000,
        (
            pltpu.VMEM((memories, slots, HD), BF16),
            pltpu.VMEM((memories, slots, HD), F32),
            pltpu.VMEM((pairs, 2 * TOK, memories * 2 * cap), BF16),
            pltpu.VMEM((memories, slots, HD), BF16),
            DMA((2, memories)),
            DMA(()),
        ),
    )


def unpack(heads):
    return call(unpack_kernel, like((TOK, heads * HD), BF16), [WHOLE], WHOLE, 40_000_000)


def body(queries, keys, values, gamma, rate, route_ids, route_weights, norm_gain):
    heads = gamma.shape[1]
    memories = rate.shape[0]
    sources = lax.axis_size("mem")
    parts = lax.axis_size("seq")
    send = pack(heads)(queries, keys, values, gamma.T, route_ids.T, route_weights.T)
    arrived = lax.all_to_all(send, "mem", 0, 0, tiled=True)
    slot_rows, update = gather(memories, sources, parts)(arrived, rate)
    pieces = lax.all_to_all(update, "seq", 0, 0, tiled=True)
    q_rows, pick = route(memories, sources)(arrived)
    pieces, q_rows, pick = lax.optimization_barrier((pieces, q_rows, pick))
    before = scan(parts)(pieces)
    raw, faded = intra(memories, sources)(slot_rows, q_rows, rate)
    state = lax.all_to_all(before, "seq", 0, 0, tiled=True).reshape(memories, HD, HD)
    gain = norm_gain.reshape(heads, HD)
    mixed = finish(memories, sources)(faded, raw, pick, state, gain)
    returned = lax.all_to_all(mixed, "mem", 0, 0, tiled=True)
    return unpack(heads)(returned)


def solution(mesh):
    split = P(("seq", "mem"), None)
    return jax.shard_map(
        body,
        mesh=mesh,
        in_specs=(split, split, split, split, P(), split, split, P()),
        out_specs=split,
        check_vma=False,
    )
```

time: 166 us -> 152 us (0.916)
  blocking collectives: 104 us -> 76.5 us
  local copies, waits for them, and re-layouts: 18.1 us -> 0.79 us
  starting transfers between devices: 5.42 us -> 15.8 us
  Pallas kernels: 38.3 us -> 48 us
  waiting for transfers between devices: 0.01 us -> 9.67 us
    all_to_all x1 -> x0, blocking collectives: 30.6 us -> none  [body(): pieces = lax.all_to_all(update, 'seq', 0, 0, tiled=True)]
    unnamed x25 -> x4, local copies, waits for them, and re-layouts: 18.1 us -> 0.79 us
    all_to_all x0 -> x1, starting transfers between devices: none -> 10.4 us  [body(): pieces = lax.all_to_all(update, 'seq', 0, 0, tiled=True)]
    all_to_all x0 -> x1, waiting for transfers between devices: none -> 9.67 us  [body(): pieces = lax.all_to_all(update, 'seq', 0, 0, tiled=True)]
    pallas_call x6 -> x7, Pallas kernels: 38.3 us -> 48 us  [the longest x1 15.6 us: body(): raw, faded = intra(memories, sources)(slot_rows, q_rows, rate)]
    all_to_all x1, blocking collectives: 50.9 us -> 52.7 us  [body(): arrived = lax.all_to_all(send, 'mem', 0, 0, tiled=True)]
  transfers between devices with their start and end apart: 1 -> 2, of which waited for: 0 -> 1; matrix products, arithmetic and copies ran while one was open for 0% -> 0% of each run, Pallas kernels for 6% -> 17%
where the time goes in v2:
time: 152 us; the launch traced here: 151 us
  blocking collectives  76.5 us (50%)
  Pallas kernels  48 us (32%)
  starting transfers between devices  15.8 us (10%)
  waiting for transfers between devices  9.67 us (6%)
    all_to_all x1, blocking collectives, body(): arrived = lax.all_to_all(send, 'mem', 0, 0, tiled=True)  52.7 us
    all_to_all x1, blocking collectives, body(): returned = lax.all_to_all(mixed, 'mem', 0, 0, tiled=True)  23.9 us
    pallas_call x1, Pallas kernels, body(): raw, faded = intra(memories, sources)(slot_rows, q_rows, rate)  15.6 us
    all_to_all x1, starting transfers between devices, body(): pieces = lax.all_to_all(update, 'seq', 0, 0, tiled=True)  10.4 us
    all_to_all x1, waiting for transfers between devices, body(): pieces = lax.all_to_all(update, 'seq', 0, 0, tiled=True)  9.67 us
    pallas_call x1, Pallas kernels, body(): q_rows, pick = route(memories, sources)(arrived)  9.33 us
    pallas_call x1, Pallas kernels, body(): mixed = finish(memories, sources)(faded, raw, pick, state, gain)  8.94 us
    pallas_call x1, Pallas kernels, body(): slot_rows, update = gather(memories, sources, parts)(arrived, rate)  8.52 us
  transfers between devices with their start and end apart: 2, of which 1 were waited for; matrix products, arithmetic and copies ran while one was open for 0% of the time, Pallas kernels for 17%

profile of v2, /device:TPU:1, one launch (start us, length us, event | category | flops | bytes accessed | tf_op | source)
XLA Modules:
  0.0 150.9 jit_solution(14587257483393989416)
XLA Ops:
  0.0 0.0 copy-start
  0.0 3.7 %shard_map.82 = bf16[16,400,128]{2,1,0:T(8,128)(2,1)} custom-call(bf16[128,2048]{1,0:T(8,128)(2,1)} %refs_0_.1, bf16[128,2048]{1,0:T(8,128)(2,1)} %refs_1_.2, bf16[128,2048]{1,0:T(8,128)(2,1)} %refs_2_.1, bf16[16,128]{1,0:T(8,128)(2,1)} %bitcast.7, s32[2,128]{1,0:T(2,128)} %bitcast.8, f32[2,128]{1,0:T(2,128)} %bitcast.9), custom_call_target="tpu_custom_call" | custom-call | tf_op jit(solution)/shard_map/pallas_call | solution.py:425
  3.7 52.7 %all_to_all.20.refs_0_ = bf16[16,400,128]{2,1,0:T(8,128)(2,1)} all-to-all(bf16[16,400,128]{2,1,0:T(8,128)(2,1)} %shard_map.82), channel_id=1, replica_groups=mesh['seq'=32,'mem'=16] {'mem'}, dimensions={0} | all-to-all | bytes 3276800 | tf_op jit(solution)/shard_map/all_to_all | solution.py:426
  56.4 0.0 copy-done
  56.4 8.5 %shard_map.83 = (bf16[16,384,256]{2,1,0:T(8,128)(2,1)}, bf16[32,80,128]{2,1,0:T(8,128)(2,1)}) custom-call(bf16[16,400,128]{2,1,0:T(8,128)(2,1)} %all_to_all.20.refs_0_, bf16[16,16]{1,0:T(8,128)(2,1)S(1)} %copy-done), custom_call_target="tpu_custom_call" | custom-call | tf_op jit(solution)/shard_map/pallas_call | solution.py:427
  64.9 10.4 %all-to-all-start.1 = ((bf16[32,80,128]{2,1,0:T(8,128)(2,1)}), bf16[32,80,128]{2,1,0:T(8,128)(2,1)S(1)}, u32[]{:S(2)}, u32[]{:S(2)}) async-start(bf16[32,80,128]{2,1,0:T(8,128)(2,1)} %get-tuple-element.15), calls=%async_computation.1 | async-start | bytes 1310720 | tf_op jit(solution)/shard_map/all_to_all | solution.py:428
  75.3 9.3 %shard_map.84 = (bf16[16,384,256]{2,1,0:T(8,128)(2,1)}, bf16[8,256,768]{2,1,0:T(8,128)(2,1)}) custom-call(bf16[16,400,128]{2,1,0:T(8,128)(2,1)} %all_to_all.20.refs_0_), custom_call_target="tpu_custom_call" | custom-call | flops 10000000000 | bytes 8388608 | tf_op jit(solution)/shard_map/pallas_call | solution.py:429
  84.6 9.7 %all-to-all-done.1.in_ref = bf16[32,80,128]{2,1,0:T(8,128)(2,1)S(1)} async-done(((bf16[32,80,128]{2,1,0:T(8,128)(2,1)}), bf16[32,80,128]{2,1,0:T(8,128)(2,1)S(1)}, u32[]{:S(2)}, u32[]{:S(2)}) %all-to-all-start.1) | async-done | bytes 655392 | tf_op jit(solution)/shard_map/all_to_all | solution.py:428
  94.3 0.9 shard_map.86
  95.2 5.4 %all-to-all-start.2 = ((bf16[32,64,128]{2,1,0:T(8,128)(2,1)}), bf16[32,64,128]{2,1,0:T(8,128)(2,1)S(1)}, u32[]{:S(2)}, u32[]{:S(2)}) async-start(bf16[32,64,128]{2,1,0:T(8,128)(2,1)} %shard_map.86), calls=%async_computation.2 | async-start | bytes 1048576 | tf_op jit(solution)/shard_map/all_to_all | solution.py:433
  100.7 15.6 %shard_map.85 = (f32[16,384,128]{2,1,0:T(8,128)}, bf16[16,384,128]{2,1,0:T(8,128)(2,1)}) custom-call(bf16[16,384,256]{2,1,0:T(8,128)(2,1)} %get-tuple-element.14.kv_ref, bf16[16,384,256]{2,1,0:T(8,128)(2,1)} %get-tuple-element.18.qg_ref, bf16[16,16]{1,0:T(8,128)(2,1)} %rate_ref.1), custom_call_target="tpu_custom_call" | custom-call | flops 10000000000 | bytes 10485760 | tf_op jit(solution)/shard_map/pallas_call | solution.py:432
  116.3 0.0 all-to-all-done.2
  116.3 0.0 copy-start.1
  116.3 0.8 copy-done.1
  117.1 8.9 %shard_map.87 = bf16[16,128,128]{2,1,0:T(8,128)(2,1)} custom-call(bf16[16,384,128]{2,1,0:T(8,128)(2,1)} %get-tuple-element.19.refs_0_, f32[16,384,128]{2,1,0:T(8,128)} %get-tuple-element.20.refs_1_, bf16[8,256,768]{2,1,0:T(8,128)(2,1)} %get-tuple-element.21.refs_2_, bf16[16,128,128]{2,1,0:T(8,128)(2,1)} %bitcast.5, f32[16,128]{1,0:T(8,128)} %bitcast.6), custom_call_target="tpu_custom_call" | custom-call | tf_op jit(solution)/shard_map/pallas_call | solution.py:435
  126.1 23.9 %all_to_all.21.in_ref = bf16[16,128,128]{2,1,0:T(8,128)(2,1)S(1)} all-to-all(bf16[16,128,128]{2,1,0:T(8,128)(2,1)} %shard_map.87), channel_id=1, replica_groups=mesh['seq'=32,'mem'=16] {'mem'}, dimensions={0} | all-to-all | bytes 1048576 | tf_op jit(solution)/shard_map/all_to_all | solution.py:436
  149.9 0.9 shard_map.88
Async XLA Ops:
  0.0 56.4 %copy-start = (bf16[16,16]{1,0:T(8,128)(2,1)S(1)}, bf16[16,16]{1,0:T(8,128)(2,1)}, u32[]{:S(2)}) copy-start(bf16[16,16]{1,0:T(8,128)(2,1)} %rate_ref.1) | copy-start | bytes 1540
  64.9 29.4 %all-to-all-start.1 = ((bf16[32,80,128]{2,1,0:T(8,128)(2,1)}), bf16[32,80,128]{2,1,0:T(8,128)(2,1)S(1)}, u32[]{:S(2)}, u32[]{:S(2)}) async-start(bf16[32,80,128]{2,1,0:T(8,128)(2,1)} %get-tuple-element.15), calls=%async_computation.1 | async-start | bytes 1310720 | tf_op jit(solution)/shard_map/all_to_all | solution.py:428
  95.2 21.1 %all-to-all-start.2 = ((bf16[32,64,128]{2,1,0:T(8,128)(2,1)}), bf16[32,64,128]{2,1,0:T(8,128)(2,1)S(1)}, u32[]{:S(2)}, u32[]{:S(2)}) async-start(bf16[32,64,128]{2,1,0:T(8,128)(2,1)} %shard_map.86), calls=%async_computation.2 | async-start | bytes 1048576 | tf_op jit(solution)/shard_map/all_to_all | solution.py:433
  116.3 0.8 copy-start.1

commit v3 on v2

v3 whole, which is shorter than its diff:
```python
import jax
import jax.numpy as jnp
from jax import lax
from jax.experimental import pallas as pl
from jax.experimental.pallas import tpu as pltpu
from jax.sharding import PartitionSpec as P

F32, BF16 = jnp.float32, jnp.bfloat16
TOK = 128
HD = 128
AUX = 16
QA = TOK + AUX
PART_ROWS = 64
EPS = 1e-6
VMEM_ALL = 58_000_000


def iota(shape, dim):
    return lax.broadcasted_iota(jnp.int32, shape, dim)


def nt(a, b):
    return lax.dot_general(a, b, (((1,), (1,)), ((), ())), preferred_element_type=F32)


def tn(a, b):
    return lax.dot_general(a, b, (((0,), (0,)), ((), ())), preferred_element_type=F32)


def dot(a, b):
    return jnp.dot(a, b, preferred_element_type=F32)


def three_parts(x):
    hi = x.astype(BF16).astype(F32)
    mid = (x - hi).astype(BF16).astype(F32)
    return hi, mid, x - hi - mid


def own_head():
    return lax.axis_index("mem")


def pack_kernel(
    heads, q_ref, k_ref, v_ref, gamma_ref, ids_ref, weights_ref, out_ref, rows_ref, sem, out_sem
):
    copies = []
    for h in range(heads):
        for at, ref in ((QA, k_ref), (QA + TOK, v_ref), (0, q_ref)):
            copies.append(
                pltpu.make_async_copy(
                    ref.at[:, h * HD : (h + 1) * HD],
                    rows_ref.at[h, at : at + TOK],
                    sem.at[len(copies)],
                )
            )
    for copy in copies:
        copy.start()
    ids = ids_ref[...]
    w_hi, w_mid, w_lo = three_parts(weights_ref[...])
    memory = iota((heads, TOK), 0)
    hit0, hit1 = memory == ids[0:1], memory == ids[1:2]
    hits = jnp.where(hit0 | hit1, 1.0, 0.0).astype(BF16)
    earlier = (iota((TOK, TOK), 0) < iota((TOK, TOK), 1)).astype(BF16)
    before = dot(hits, earlier)
    rank0 = jnp.sum(jnp.where(hit0, before, 0.0), axis=0, keepdims=True)
    rank1 = jnp.sum(jnp.where(hit1, before, 0.0), axis=0, keepdims=True)
    row = iota((AUX, TOK), 0)
    shared = jnp.zeros((AUX, TOK), F32)
    entries = [ids[0:1].astype(F32), rank0, ids[1:2].astype(F32), rank1]
    for part in (w_hi, w_mid, w_lo):
        entries += [part[0:1], part[1:2]]
    for at, entry in enumerate(entries):
        shared = jnp.where(row == at + 1, entry, shared)
    gamma_rows = gamma_ref[...].astype(F32)
    for h in range(heads):
        aux = jnp.where(row == 0, gamma_rows[h : h + 1], shared)
        rows_ref[h, TOK:QA] = aux.astype(BF16)
    leaving = []
    for h in range(heads):
        for copy in copies[3 * h : 3 * h + 3]:
            copy.wait()
        leaving.append(pltpu.make_async_copy(rows_ref.at[h], out_ref.at[h], out_sem.at[h]))
        leaving[h].start()
    for copy in leaving:
        copy.wait()


def head_rates(rate_ref, head, scratch_ref):
    rates = rate_ref[...].astype(F32)
    mine = jnp.where(iota(rates.shape, 1) == head, rates, 0.0)
    scratch_ref[...] = jnp.broadcast_to(jnp.sum(mine, axis=1, keepdims=True), scratch_ref.shape)


def slot_ids(aux, cap, side):
    at = aux[0:8].astype(jnp.int32)
    first = at[1:2] * (2 * cap) + at[2:3] + side * cap
    second = at[3:4] * (2 * cap) + at[4:5] + side * cap
    return first, second


def gather_kernel(
    cap, in_ref, rate_ref, slots_out, update_out, aux_ref, rows_ref, slots_ref, rest_ref, update_ref, rates_ref, later_ref, sem, aux_sem, slots_sem, update_sem
):
    sources = in_ref.shape[0]
    memories, slots, _ = slots_ref.shape
    width = memories * 2 * cap

    def arriving(source):
        return pltpu.make_async_copy(
            in_ref.at[source, QA : QA + 2 * TOK], rows_ref.at[source], sem.at[source]
        )

    small = pltpu.make_async_copy(in_ref.at[:, TOK:QA], aux_ref, aux_sem)
    small.start()
    for source in range(sources):
        arriving(source).start()
    head_rates(rate_ref, own_head(), rates_ref)
    after = (iota((TOK, TOK), 0) > iota((TOK, TOK), 1)).astype(BF16)
    memory = iota((memories, TOK), 0)
    small.wait()

    hits, gammas = [], []
    for source in range(sources):
        aux = aux_ref[source].astype(F32)
        at = aux.astype(jnp.int32)
        hit = (memory == at[1:2]) | (memory == at[3:4])
        gammas.append(jnp.where(hit, aux[0:1], 0.0))
    inside = dot(jnp.concatenate(gammas, axis=0).astype(BF16), after)
    behind = jnp.zeros((memories, 1), F32)
    for source in reversed(range(sources)):
        own = inside[source * memories : (source + 1) * memories]
        later_ref[source] = own + behind
        behind = behind + own[:, 0:1] + gammas[source][:, 0:1]
    total = -rates_ref[...] * behind

    place = iota((width, TOK), 0)

    def gather(pair, carry):
        rows, select, rest = [], [], jnp.zeros((width, TOK), F32)
        for side in range(2):
            source = 2 * pair + side
            arriving(source).wait()
            aux = aux_ref[source].astype(F32)
            at = aux.astype(jnp.int32)
            later = later_ref[source]
            rest0 = jnp.sum(jnp.where(memory == at[1:2], later, 0.0), axis=0, keepdims=True)
            rest1 = jnp.sum(jnp.where(memory == at[3:4], later, 0.0), axis=0, keepdims=True)
            first, second = slot_ids(aux, cap, side)
            hit0, hit1 = place == first, place == second
            select.append(jnp.where(hit0 | hit1, 1.0, 0.0).astype(BF16))
            rest = rest + jnp.where(hit0, rest0, jnp.where(hit1, rest1, 0.0))
            rows.append(
                jnp.concatenate([rows_ref[source, 0:TOK], rows_ref[source, TOK : 2 * TOK]], axis=1)
            )
        rest = jnp.broadcast_to(jnp.sum(rest, axis=1, keepdims=True), (width, HD))
        got = dot(jnp.concatenate(select, axis=1), jnp.concatenate(rows, axis=0)).astype(BF16)
        at = pl.ds(pl.multiple_of(pair * 2 * cap, 2 * cap), 2 * cap)
        for m in range(memories):
            slots_ref[m, at, :] = got[m * 2 * cap : (m + 1) * 2 * cap]
            rest_ref[m, at, :] = rest[m * 2 * cap : (m + 1) * 2 * cap]
        leaving(pair).start()
        return carry

    def leaving(pair):
        at = pl.ds(pl.multiple_of(pair * 2 * cap, 2 * cap), 2 * cap)
        return pltpu.make_async_copy(slots_ref.at[:, at], slots_out.at[:, at], slots_sem.at[pair])

    lax.fori_loop(0, sources // 2, gather, 0)

    row = iota((AUX, HD), 0)
    for m in range(memories):
        aux = jnp.zeros((AUX, HD), F32)
        for at, part in enumerate(three_parts(total[m : m + 1])):
            aux = jnp.where(row == at, part, aux)
        for half in range(2):
            update_ref[2 * m + half, PART_ROWS : PART_ROWS + AUX] = aux.astype(BF16)

    def updated(step):
        at = pl.ds(step * 8, 8)
        return pltpu.make_async_copy(update_ref.at[at], update_out.at[at], update_sem.at[step])

    def update(step, carry):
        for m in range(4):
            m = 4 * step + m
            k = slots_ref[m, :, 0:HD].astype(F32)
            v = slots_ref[m, :, HD : 2 * HD]
            kd = (k * jnp.exp(-rates_ref[pl.ds(m, 1), :] * rest_ref[m])).astype(BF16)
            added = tn(kd, v).astype(BF16)
            for half in range(2):
                part = added[half * PART_ROWS : (half + 1) * PART_ROWS]
                update_ref[2 * m + half, 0:PART_ROWS] = part
        updated(step).start()
        return carry

    lax.fori_loop(0, memories // 4, update, 0)
    for step in range(memories // 4):
        updated(step).wait()
    for pair in range(sources // 2):
        leaving(pair).wait()


def scan_kernel(in_ref, out_ref):
    state = jnp.zeros((PART_ROWS, HD), F32)
    for part in range(in_ref.shape[0]):
        out_ref[part] = state.astype(BF16)
        aux = in_ref[part, PART_ROWS : PART_ROWS + AUX].astype(F32)
        fade = jnp.exp(aux[0:1] + aux[1:2] + aux[2:3])
        state = fade * state + in_ref[part, 0:PART_ROWS].astype(F32)


def beside_kernel(
    cap,
    in_hbm,
    kv_hbm,
    rate_ref,
    raw_hbm,
    faded_hbm,
    pick_hbm,
    rows_ref,
    kv_ref,
    qg_ref,
    raw_ref,
    faded_ref,
    pick_ref,
    rates_ref,
    sums_ref,
    rows_sem,
    kv_sem,
    pick_sem,
    raw_sem,
    faded_sem,
):
    memories, slots, _ = kv_ref.shape
    pairs = pick_ref.shape[0]
    width = memories * 2 * cap

    def rows_in(pair):
        two = pl.ds(2 * pair, 2)
        return pltpu.make_async_copy(in_hbm.at[two, 0:QA], rows_ref.at[two], rows_sem.at[pair])

    def kv_in(step):
        four = pl.ds(4 * step, 4)
        return pltpu.make_async_copy(kv_hbm.at[four], kv_ref.at[four], kv_sem.at[step])

    def pick_out(pair):
        return pltpu.make_async_copy(pick_ref.at[pair], pick_hbm.at[pair], pick_sem.at[pair])

    def made_out(step):
        two = pl.ds(2 * step, 2)
        return (
            pltpu.make_async_copy(raw_ref.at[two], raw_hbm.at[two], raw_sem.at[step]),
            pltpu.make_async_copy(faded_ref.at[two], faded_hbm.at[two], faded_sem.at[step]),
        )

    for pair in range(pairs):
        rows_in(pair).start()
    for step in range(memories // 4):
        kv_in(step).start()
    head_rates(rate_ref, own_head(), rates_ref)
    tri = iota((TOK, TOK), 0) - iota((TOK, TOK), 1)
    sums_ref[0:TOK] = (tri >= 0).astype(BF16)
    sums_ref[TOK : 2 * TOK] = (tri < 0).astype(BF16)
    ones = jnp.ones((TOK, HD), BF16)
    eye = (tri == 0).astype(BF16)
    down, across = iota((width, TOK), 0), iota((TOK, width), 1)

    def route(pair, carry):
        rows_in(pair).wait()
        rows, select = [], []
        for side in range(2):
            packed = rows_ref[2 * pair + side, TOK:QA]
            aux = packed.astype(F32)
            gamma = dot(jnp.where(tri == 0, aux[0:1], 0.0).astype(BF16), ones).astype(BF16)
            rows.append(jnp.concatenate([rows_ref[2 * pair + side, 0:TOK], gamma], axis=1))
            first, second = slot_ids(aux, cap, side)
            hit = (down == first) | (down == second)
            select.append(jnp.where(hit, 1.0, 0.0).astype(BF16))
            aux = nt(eye, packed)
            at = aux.astype(jnp.int32)
            first = at[:, 1:2] * (2 * cap) + at[:, 2:3] + side * cap
            second = at[:, 3:4] * (2 * cap) + at[:, 4:5] + side * cap
            w0 = aux[:, 5:6] + aux[:, 7:8] + aux[:, 9:10]
            w1 = aux[:, 6:7] + aux[:, 8:9] + aux[:, 10:11]
            pick = jnp.where(across == first, w0, jnp.where(across == second, w1, 0.0))
            pick_ref[pair, side * TOK : (side + 1) * TOK] = pick.astype(BF16)
        pick_out(pair).start()
        got = dot(jnp.concatenate(select, axis=1), jnp.concatenate(rows, axis=0)).astype(BF16)
        at = pl.ds(pl.multiple_of(pair * 2 * cap, 2 * cap), 2 * cap)
        for m in range(memories):
            qg_ref[m, at, :] = got[m * 2 * cap : (m + 1) * 2 * cap]
        return carry

    lax.fori_loop(0, pairs, route, 0, unroll=1)
    for step in range(memories // 4):
        kv_in(step).wait()

    def intra(step, carry):
        for m in (2 * step, 2 * step + 1):
            rate = rates_ref[pl.ds(m, 1), :]
            behind = []
            faded_all = jnp.ones((1, HD), F32)
            for b in range(slots // TOK):
                at = slice(b * TOK, (b + 1) * TOK)
                seen = slice(0, (b + 1) * TOK)
                q = qg_ref[m, at, 0:HD]
                gamma = qg_ref[m, at, HD : 2 * HD]
                masked = jnp.where(tri > 0, gamma.astype(F32), 0.0).astype(BF16)
                sums = dot(sums_ref[...], jnp.concatenate([masked, gamma], axis=1))
                inside = jnp.where(tri >= 0, jnp.exp(-rate * sums[0:TOK, 0:TOK]), 0.0)
                fade = jnp.exp(-rate * sums[0:TOK, TOK : 2 * TOK])
                faded_ref[m, at] = (q.astype(F32) * (fade * faded_all)).astype(BF16)
                decay = jnp.concatenate([fade * row for row in behind] + [inside], axis=1)
                weights = (decay * nt(q, kv_ref[m, seen, 0:HD])).astype(BF16)
                raw_ref[m, at] = dot(weights, kv_ref[m, seen, HD : 2 * HD])
                if (b + 1) * TOK < slots:
                    whole = fade[TOK - 1 : TOK]
                    faded_all = faded_all * whole
                    rest = jnp.exp(-rate * sums[TOK : 2 * TOK, TOK : 2 * TOK])
                    behind = [row * whole for row in behind] + [rest.T]
        for copy in made_out(step):
            copy.start()
        return carry

    lax.fori_loop(0, memories // 2, intra, 0, unroll=1)
    for pair in range(pairs):
        pick_out(pair).wait()
    for step in range(memories // 2):
        for copy in made_out(step):
            copy.wait()


def finish_kernel(cap, faded_ref, raw_ref, pick_ref, state_ref, gain_ref, out_ref, made_ref):
    memories = faded_ref.shape[0]

    def one(m, carry):
        raw = raw_ref[m] + dot(faded_ref[m], state_ref[m])
        mean = jnp.mean(raw * raw, axis=1, keepdims=True)
        made_ref[m] = (raw * lax.rsqrt(mean + EPS)).astype(BF16)
        return carry

    lax.fori_loop(0, memories, one, 0, unroll=4)
    gain = gain_ref[pl.ds(own_head(), 1), :]

    def mix(pair, carry):
        at = pl.ds(pl.multiple_of(pair * 2 * cap, 2 * cap), 2 * cap)
        rows = jnp.concatenate([made_ref[m, at, :] for m in range(memories)], axis=0)
        mixed = (gain * dot(pick_ref[pair], rows)).astype(BF16)
        for side in range(2):
            out_ref[2 * pair + side] = mixed[side * TOK : (side + 1) * TOK]
        return carry

    lax.fori_loop(0, pick_ref.shape[0], mix, 0, unroll=4)


def unpack_kernel(in_ref, out_ref):
    for h in range(in_ref.shape[0]):
        out_ref[:, h * HD : (h + 1) * HD] = in_ref[h]


like = jax.ShapeDtypeStruct
ANY = pl.BlockSpec(memory_space=pl.ANY)
WHOLE = pl.BlockSpec(memory_space=pltpu.VMEM)
DMA = pltpu.SemaphoreType.DMA


def call(kernel, outs, ins, out_specs, room, scratch=(), grid=(), flops=0, moved=0):
    return pl.pallas_call(
        kernel,
        out_shape=outs,
        grid=grid,
        in_specs=ins,
        out_specs=out_specs,
        scratch_shapes=list(scratch),
        compiler_params=pltpu.CompilerParams(vmem_limit_bytes=VMEM_ALL - room),
        cost_estimate=pl.CostEstimate(flops=flops, bytes_accessed=moved, transcendentals=0),
    )


def pack(heads):
    return call(
        lambda *refs: pack_kernel(heads, *refs),
        like((heads, QA + 2 * TOK, HD), BF16),
        [ANY, ANY, ANY, WHOLE, WHOLE, WHOLE],
        ANY,
        -2_000_000,
        (
            pltpu.VMEM((heads, QA + 2 * TOK, HD), BF16),
            DMA((3 * heads,)),
            DMA((heads,)),
        ),
    )


def gather(memories, sources, parts):
    cap = 3 * TOK // memories
    slots = sources * cap
    return call(
        lambda *refs: gather_kernel(cap, *refs),
        (
            like((memories, slots, 2 * HD), BF16),
            like((parts, PART_ROWS + AUX, HD), BF16),
        ),
        [ANY, WHOLE],
        (ANY, ANY),
        -2_000_000,
        (
            pltpu.VMEM((sources, AUX, TOK), BF16),
            pltpu.VMEM((sources, 2 * TOK, HD), BF16),
            pltpu.VMEM((memories, slots, 2 * HD), BF16),
            pltpu.VMEM((memories, slots, HD), F32),
            pltpu.VMEM((parts, PART_ROWS + AUX, HD), BF16),
            pltpu.VMEM((memories, HD), F32),
            pltpu.VMEM((sources, memories, TOK), F32),
            DMA((sources,)),
            DMA(()),
            DMA((sources // 2,)),
            DMA((memories // 4,)),
        ),
    )


def scan(parts):
    return call(
        scan_kernel,
        like((parts, PART_ROWS, HD), BF16),
        [WHOLE],
        WHOLE,
        40_000_000,
        flops=2 * 10**10,
        moved=2**20,
    )


def beside(memories, sources):
    cap = 3 * TOK // memories
    slots = sources * cap
    pairs = sources // 2
    pick = (pairs, 2 * TOK, memories * 2 * cap)
    return call(
        lambda *refs: beside_kernel(cap, *refs),
        (like((memories, slots, HD), F32), like((memories, slots, HD), BF16), like(pick, BF16)),
        [ANY, ANY, WHOLE],
        (ANY, ANY, ANY),
        -2_000_000,
        (
            pltpu.VMEM((sources, QA, HD), BF16),
            pltpu.VMEM((memories, slots, 2 * HD), BF16),
            pltpu.VMEM((memories, slots, 2 * HD), BF16),
            pltpu.VMEM((memories, slots, HD), F32),
            pltpu.VMEM((memories, slots, HD), BF16),
            pltpu.VMEM(pick, BF16),
            pltpu.VMEM((memories, HD), F32),
            pltpu.VMEM((2 * TOK, TOK), BF16),
            DMA((pairs,)),
            DMA((memories // 4,)),
            DMA((pairs,)),
            DMA((memories // 2,)),
            DMA((memories // 2,)),
        ),
        flops=15 * 10**9,
        moved=12 * 2**20,
    )


def finish(memories, sources):
    cap = 3 * TOK // memories
    slots = sources * cap
    return call(
        lambda *refs: finish_kernel(cap, *refs),
        like((sources, TOK, HD), BF16),
        [WHOLE] * 5,
        WHOLE,
        40_000_000,
        (pltpu.VMEM((memories, slots, HD), BF16),),
    )


def unpack(heads):
    return call(unpack_kernel, like((TOK, heads * HD), BF16), [WHOLE], WHOLE, 40_000_000)


def body(queries, keys, values, gamma, rate, route_ids, route_weights, norm_gain):
    heads = gamma.shape[1]
    memories = rate.shape[0]
    sources = lax.axis_size("mem")
    parts = lax.axis_size("seq")
    send = pack(heads)(queries, keys, values, gamma.T, route_ids.T, route_weights.T)
    arrived = lax.all_to_all(send, "mem", 0, 0, tiled=True)
    slot_rows, update = gather(memories, sources, parts)(arrived, rate)
    pieces = lax.all_to_all(update, "seq", 0, 0, tiled=True)
    raw, faded, pick = beside(memories, sources)(arrived, slot_rows, rate)
    pieces, raw, faded, pick = lax.optimization_barrier((pieces, raw, faded, pick))
    before = scan(parts)(pieces)
    state = lax.all_to_all(before, "seq", 0, 0, tiled=True).reshape(memories, HD, HD)
    gain = norm_gain.reshape(heads, HD)
    mixed = finish(memories, sources)(faded, raw, pick, state, gain)
    returned = lax.all_to_all(mixed, "mem", 0, 0, tiled=True)
    return unpack(heads)(returned)


def solution(mesh):
    split = P(("seq", "mem"), None)
    return jax.shard_map(
        body,
        mesh=mesh,
        in_specs=(split, split, split, split, P(), split, split, P()),
        out_specs=split,
        check_vma=False,
    )
```

time: 152 us -> 143 us (0.941)
  blocking collectives: 76.5 us -> 97.5 us
  Pallas kernels: 48 us -> 32 us
  waiting for transfers between devices: 9.67 us -> 3 us
  starting transfers between devices: 15.8 us -> 10.4 us
    all_to_all x0 -> x1, blocking collectives: none -> 22.2 us  [body(): lax.all_to_all(before, 'seq', 0, 0, tiled=True).reshape(memories, HD, HD)]
    pallas_call x2 -> x1, Pallas kernels: 25 us -> 16 us  [body(): raw, faded, pick = beside(memories, sources)(arrived, slot_rows, rate)]
    all_to_all x1, waiting for transfers between devices: 9.67 us -> 3 us  [body(): pieces = lax.all_to_all(update, 'seq', 0, 0, tiled=True)]
    pallas_call x1, Pallas kernels: 8.94 us -> 2.95 us  [body(): mixed = finish(memories, sources)(faded, raw, pick, state, gain)]
    all_to_all x1 -> x0, starting transfers between devices: 5.42 us -> none  [body(): lax.all_to_all(before, 'seq', 0, 0, tiled=True).reshape(memories, HD, HD)]
  transfers between devices with their start and end apart: 2 -> 1, of which waited for: 1 -> 1; matrix products, arithmetic and copies ran while one was open for 0% -> 0% of each run, Pallas kernels for 17% -> 11%
where the time goes in v3:
time: 143 us
  blocking collectives  97.5 us (68%)
  Pallas kernels  32 us (22%)
  starting transfers between devices  10.4 us (7%)
  waiting for transfers between devices  3 us (2%)
    all_to_all x1, blocking collectives, body(): arrived = lax.all_to_all(send, 'mem', 0, 0, tiled=True)  52.7 us
    all_to_all x1, blocking collectives, body(): returned = lax.all_to_all(mixed, 'mem', 0, 0, tiled=True)  22.6 us
    all_to_all x1, blocking collectives, body(): lax.all_to_all(before, 'seq', 0, 0, tiled=True).reshape(memories, HD, HD)  22.2 us
    pallas_call x1, Pallas kernels, body(): raw, faded, pick = beside(memories, sources)(arrived, slot_rows, rate)  16 us
    all_to_all x1, starting transfers between devices, body(): pieces = lax.all_to_all(update, 'seq', 0, 0, tiled=True)  10.4 us
    pallas_call x1, Pallas kernels, body(): slot_rows, update = gather(memories, sources, parts)(arrived, rate)  8.59 us
    pallas_call x1, Pallas kernels, body(): pack(heads)(queries, keys, values, gamma.T, route_ids.T, route_weights.T)  3.34 us
    all_to_all x1, waiting for transfers between devices, body(): pieces = lax.all_to_all(update, 'seq', 0, 0, tiled=True)  3 us
  transfers between devices with their start and end apart: 1, of which 1 were waited for; matrix products, arithmetic and copies ran while one was open for 0% of the time, Pallas kernels for 11%

profile of v3, /device:TPU:1, one launch (start us, length us, event | category | flops | bytes accessed | tf_op | source)
XLA Modules:
  0.0 142.9 jit_solution(9352434782986794254)
XLA Ops:
  0.0 3.3 %shard_map.82 = bf16[16,400,128]{2,1,0:T(8,128)(2,1)} custom-call(bf16[128,2048]{1,0:T(8,128)(2,1)} %refs_0_.1, bf16[128,2048]{1,0:T(8,128)(2,1)} %refs_1_.2, bf16[128,2048]{1,0:T(8,128)(2,1)} %refs_2_.2, bf16[16,128]{1,0:T(8,128)(2,1)} %bitcast.7, s32[2,128]{1,0:T(2,128)} %bitcast.8, f32[2,128]{1,0:T(2,128)} %bitcast.9), custom_call_target="tpu_custom_call" | custom-call | tf_op jit(solution)/shard_map/pallas_call | solution.py:488
  3.3 52.7 %all_to_all.20.refs_0_ = bf16[16,400,128]{2,1,0:T(8,128)(2,1)} all-to-all(bf16[16,400,128]{2,1,0:T(8,128)(2,1)} %shard_map.82), channel_id=1, replica_groups=mesh['seq'=32,'mem'=16] {'mem'}, dimensions={0} | all-to-all | bytes 3276800 | tf_op jit(solution)/shard_map/all_to_all | solution.py:489
  56.0 8.6 %shard_map.83 = (bf16[16,384,256]{2,1,0:T(8,128)(2,1)}, bf16[32,80,128]{2,1,0:T(8,128)(2,1)}) custom-call(bf16[16,400,128]{2,1,0:T(8,128)(2,1)} %all_to_all.20.refs_0_, bf16[16,16]{1,0:T(8,128)(2,1)} %refs_2_.3), custom_call_target="tpu_custom_call" | custom-call | tf_op jit(solution)/shard_map/pallas_call | solution.py:490
  64.6 10.4 %all-to-all-start.1 = ((bf16[32,80,128]{2,1,0:T(8,128)(2,1)}), bf16[32,80,128]{2,1,0:T(8,128)(2,1)S(1)}, u32[]{:S(2)}, u32[]{:S(2)}) async-start(bf16[32,80,128]{2,1,0:T(8,128)(2,1)} %get-tuple-element.14), calls=%async_computation.1 | async-start | bytes 1310720 | tf_op jit(solution)/shard_map/all_to_all | solution.py:491
  75.0 16.0 %shard_map.84 = (f32[16,384,128]{2,1,0:T(8,128)}, bf16[16,384,128]{2,1,0:T(8,128)(2,1)}, bf16[8,256,768]{2,1,0:T(8,128)(2,1)}) custom-call(bf16[16,400,128]{2,1,0:T(8,128)(2,1)} %all_to_all.20.refs_0_, bf16[16,384,256]{2,1,0:T(8,128)(2,1)} %get-tuple-element.15.refs_1_, bf16[16,16]{1,0:T(8,128)(2,1)} %refs_2_.3), custom_call_target="tpu_custom_call" | custom-call | flops 15000000512 | bytes 12582912 | tf_op jit(solution)/shard_map/pallas_call | solution.py:492
  91.0 3.0 %all-to-all-done.1.in_ref = bf16[32,80,128]{2,1,0:T(8,128)(2,1)S(1)} async-done(((bf16[32,80,128]{2,1,0:T(8,128)(2,1)}), bf16[32,80,128]{2,1,0:T(8,128)(2,1)S(1)}, u32[]{:S(2)}, u32[]{:S(2)}) %all-to-all-start.1) | async-done | bytes 655392 | tf_op jit(solution)/shard_map/all_to_all | solution.py:491
  94.0 0.0 copy-start
  94.0 0.0 copy-start.1
  94.0 0.0 copy-start.2
  94.0 0.0 copy-start.3
  94.0 0.2 shard_map.85
  94.2 22.2 %all_to_all.21 = bf16[32,64,128]{2,1,0:T(8,128)(2,1)S(1)} all-to-all(bf16[32,64,128]{2,1,0:T(8,128)(2,1)S(1)} %shard_map.85), channel_id=1, replica_groups=mesh['seq'=32,'mem'=16] {'seq'}, dimensions={0} | all-to-all | bytes 1048576 | tf_op jit(solution)/shard_map/all_to_all | solution.py:495
  116.4 0.0 copy-done
  116.4 0.0 copy-done.1
  116.4 0.0 copy-done.2
  116.4 0.0 copy-done.3
  116.4 2.9 %shard_map.86 = bf16[16,128,128]{2,1,0:T(8,128)(2,1)S(1)} custom-call(bf16[16,384,128]{2,1,0:T(8,128)(2,1)S(1)} %copy-done.2, f32[16,384,128]{2,1,0:T(8,128)S(1)} %copy-done, bf16[8,256,768]{2,1,0:T(8,128)(2,1)S(1)} %copy-done.1, bf16[16,128,128]{2,1,0:T(8,128)(2,1)S(1)} %bitcast.5, f32[16,128]{1,0:T(8,128)S(1)} %bitcast.6), custom_call_target="tpu_custom_call" | custom-call | tf_op jit(solution)/shard_map/pallas_call | solution.py:497
  119.3 22.6 %all_to_all.22.in_ref = bf16[16,128,128]{2,1,0:T(8,128)(2,1)S(1)} all-to-all(bf16[16,128,128]{2,1,0:T(8,128)(2,1)S(1)} %shard_map.86), channel_id=1, replica_groups=mesh['seq'=32,'mem'=16] {'mem'}, dimensions={0} | all-to-all | bytes 1048576 | tf_op jit(solution)/shard_map/all_to_all | solution.py:498
  141.9 0.9 shard_map.87
Async XLA Ops:
  64.6 29.4 %all-to-all-start.1 = ((bf16[32,80,128]{2,1,0:T(8,128)(2,1)}), bf16[32,80,128]{2,1,0:T(8,128)(2,1)S(1)}, u32[]{:S(2)}, u32[]{:S(2)}) async-start(bf16[32,80,128]{2,1,0:T(8,128)(2,1)} %get-tuple-element.14), calls=%async_computation.1 | async-start | bytes 1310720 | tf_op jit(solution)/shard_map/all_to_all | solution.py:491
  94.0 22.4 %copy-start = (f32[16,384,128]{2,1,0:T(8,128)S(1)}, f32[16,384,128]{2,1,0:T(8,128)}, u32[]{:S(2)}) copy-start(f32[16,384,128]{2,1,0:T(8,128)} %get-tuple-element.20.refs_1_) | copy-start | bytes 9437188
  94.0 22.4 %copy-start.1 = (bf16[8,256,768]{2,1,0:T(8,128)(2,1)S(1)}, bf16[8,256,768]{2,1,0:T(8,128)(2,1)}, u32[]{:S(2)}) copy-start(bf16[8,256,768]{2,1,0:T(8,128)(2,1)} %get-tuple-element.21.refs_2_) | copy-start | bytes 9437188
  94.0 22.4 %copy-start.2 = (bf16[16,384,128]{2,1,0:T(8,128)(2,1)S(1)}, bf16[16,384,128]{2,1,0:T(8,128)(2,1)}, u32[]{:S(2)}) copy-start(bf16[16,384,128]{2,1,0:T(8,128)(2,1)} %get-tuple-element.19.refs_0_) | copy-start | bytes 4718596
  94.0 22.4 %copy-start.3 = (f32[2048]{0:T(1024)S(1)}, f32[2048]{0:T(1024)}, u32[]{:S(2)}) copy-start(f32[2048]{0:T(1024)} %param.15) | copy-start | bytes 24580

commit v4 on v3

--- a/solution.py
+++ b/solution.py
@@ -11,8 +11,10 @@
 AUX = 16
 QA = TOK + AUX
 PART_ROWS = 64
+GROUPS = 2
 EPS = 1e-6
 VMEM_ALL = 58_000_000
+ROOM = 4_900_000
 
 
 def iota(shape, dim):
@@ -42,20 +44,29 @@
 
 
 def pack_kernel(
-    heads, q_ref, k_ref, v_ref, gamma_ref, ids_ref, weights_ref, out_ref, rows_ref, sem, out_sem
+    heads, q_ref, k_ref, v_ref, gamma_hbm, ids_hbm, weights_hbm, out_ref, gamma_ref, ids_ref, weights_ref, given_ref, rows_ref, small_sem, sem, out_sem
 ):
-    copies = []
-    for h in range(heads):
-        for at, ref in ((QA, k_ref), (QA + TOK, v_ref), (0, q_ref)):
-            copies.append(
-                pltpu.make_async_copy(
-                    ref.at[:, h * HD : (h + 1) * HD],
-                    rows_ref.at[h, at : at + TOK],
-                    sem.at[len(copies)],
-                )
-            )
-    for copy in copies:
+    groups, lanes = out_sem.shape[0], heads * HD // out_sem.shape[0]
+
+    def arriving(group):
+        at = slice(group * lanes, (group + 1) * lanes)
+        return [
+            pltpu.make_async_copy(ref.at[:, at], given_ref.at[which, :, at], sem.at[which, group])
+            for which, ref in enumerate((q_ref, k_ref, v_ref))
+        ]
+
+    small = [
+        pltpu.make_async_copy(gamma_hbm, gamma_ref, small_sem.at[0]),
+        pltpu.make_async_copy(ids_hbm, ids_ref, small_sem.at[1]),
+        pltpu.make_async_copy(weights_hbm, weights_ref, small_sem.at[2]),
+    ]
+    for copy in small:
         copy.start()
+    for group in range(groups):
+        for copy in arriving(group):
+            copy.start()
+    for copy in small:
+        copy.wait()
     ids = ids_ref[...]
     w_hi, w_mid, w_lo = three_parts(weights_ref[...])
     memory = iota((heads, TOK), 0)
@@ -77,11 +88,16 @@
         aux = jnp.where(row == 0, gamma_rows[h : h + 1], shared)
         rows_ref[h, TOK:QA] = aux.astype(BF16)
     leaving = []
-    for h in range(heads):
-        for copy in copies[3 * h : 3 * h + 3]:
+    for group in range(groups):
+        for copy in arriving(group):
             copy.wait()
-        leaving.append(pltpu.make_async_copy(rows_ref.at[h], out_ref.at[h], out_sem.at[h]))
-        leaving[h].start()
+        some = range(group * heads // groups, (group + 1) * heads // groups)
+        for h in some:
+            for which, at in enumerate((0, QA, QA + TOK)):
+                rows_ref[h, at : at + TOK] = given_ref[which, :, h * HD : (h + 1) * HD]
+        at = pl.ds(some[0], len(some))
+        leaving.append(pltpu.make_async_copy(rows_ref.at[at], out_ref.at[at], out_sem.at[group]))
+        leaving[group].start()
     for copy in leaving:
         copy.wait()
 
@@ -92,37 +108,30 @@
     scratch_ref[...] = jnp.broadcast_to(jnp.sum(mine, axis=1, keepdims=True), scratch_ref.shape)
 
 
-def slot_ids(aux, cap, side):
+def own_slots(aux, cap):
     at = aux[0:8].astype(jnp.int32)
-    first = at[1:2] * (2 * cap) + at[2:3] + side * cap
-    second = at[3:4] * (2 * cap) + at[4:5] + side * cap
-    return first, second
+    return at[1:2] * cap + at[2:3], at[3:4] * cap + at[4:5]
+
+
+def spread(rows, cap, side):
+    parts = rows.reshape(-1, cap, rows.shape[1])
+    parts = [parts, jnp.zeros_like(parts)][:: 1 - 2 * side]
+    return jnp.concatenate(parts, axis=1).reshape(-1, rows.shape[1])
 
 
 def gather_kernel(
-    cap, in_ref, rate_ref, slots_out, update_out, aux_ref, rows_ref, slots_ref, rest_ref, update_ref, rates_ref, later_ref, sem, aux_sem, slots_sem, update_sem
+    cap, in_ref, rate_ref, slots_out, update_out, slots_ref, rest_ref, update_ref, rates_ref, later_ref, slots_sem, update_sem
 ):
     sources = in_ref.shape[0]
     memories, slots, _ = slots_ref.shape
     width = memories * 2 * cap
 
-    def arriving(source):
-        return pltpu.make_async_copy(
-            in_ref.at[source, QA : QA + 2 * TOK], rows_ref.at[source], sem.at[source]
-        )
-
-    small = pltpu.make_async_copy(in_ref.at[:, TOK:QA], aux_ref, aux_sem)
-    small.start()
-    for source in range(sources):
-        arriving(source).start()
     head_rates(rate_ref, own_head(), rates_ref)
     after = (iota((TOK, TOK), 0) > iota((TOK, TOK), 1)).astype(BF16)
     memory = iota((memories, TOK), 0)
-    small.wait()
-
     hits, gammas = [], []
     for source in range(sources):
-        aux = aux_ref[source].astype(F32)
+        aux = in_ref[source, TOK:QA].astype(F32)
         at = aux.astype(jnp.int32)
         hit = (memory == at[1:2]) | (memory == at[3:4])
         gammas.append(jnp.where(hit, aux[0:1], 0.0))
@@ -134,31 +143,31 @@
         behind = behind + own[:, 0:1] + gammas[source][:, 0:1]
     total = -rates_ref[...] * behind
 
-    place = iota((width, TOK), 0)
+    place = iota((width // 2, TOK), 0)
 
     def gather(pair, carry):
-        rows, select, rest = [], [], jnp.zeros((width, TOK), F32)
+        rows, select, rest = [], [], []
         for side in range(2):
             source = 2 * pair + side
-            arriving(source).wait()
-            aux = aux_ref[source].astype(F32)
+            aux = in_ref[source, TOK:QA].astype(F32)
             at = aux.astype(jnp.int32)
             later = later_ref[source]
             rest0 = jnp.sum(jnp.where(memory == at[1:2], later, 0.0), axis=0, keepdims=True)
             rest1 = jnp.sum(jnp.where(memory == at[3:4], later, 0.0), axis=0, keepdims=True)
-            first, second = slot_ids(aux, cap, side)
+            first, second = own_slots(aux, cap)
             hit0, hit1 = place == first, place == second
-            select.append(jnp.where(hit0 | hit1, 1.0, 0.0).astype(BF16))
-            rest = rest + jnp.where(hit0, rest0, jnp.where(hit1, rest1, 0.0))
-            rows.append(
-                jnp.concatenate([rows_ref[source, 0:TOK], rows_ref[source, TOK : 2 * TOK]], axis=1)
-            )
-        rest = jnp.broadcast_to(jnp.sum(rest, axis=1, keepdims=True), (width, HD))
+            select.append(spread(jnp.where(hit0 | hit1, 1.0, 0.0), cap, side).astype(BF16))
+            own = jnp.where(hit0, rest0, jnp.where(hit1, rest1, 0.0))
+            own = jnp.broadcast_to(jnp.sum(own, axis=1, keepdims=True), own.shape)
+            rest.append(own.reshape(memories, cap, TOK))
+            k, v = in_ref[source, QA : QA + TOK], in_ref[source, QA + TOK : QA + 2 * TOK]
+            rows.append(jnp.concatenate([k, v], axis=1))
+        rest = jnp.concatenate(rest, axis=1)
         got = dot(jnp.concatenate(select, axis=1), jnp.concatenate(rows, axis=0)).astype(BF16)
         at = pl.ds(pl.multiple_of(pair * 2 * cap, 2 * cap), 2 * cap)
         for m in range(memories):
             slots_ref[m, at, :] = got[m * 2 * cap : (m + 1) * 2 * cap]
-            rest_ref[m, at, :] = rest[m * 2 * cap : (m + 1) * 2 * cap]
+            rest_ref[m, at, :] = rest[m]
         leaving(pair).start()
         return carry
 
@@ -166,7 +175,7 @@
         at = pl.ds(pl.multiple_of(pair * 2 * cap, 2 * cap), 2 * cap)
         return pltpu.make_async_copy(slots_ref.at[:, at], slots_out.at[:, at], slots_sem.at[pair])
 
-    lax.fori_loop(0, sources // 2, gather, 0)
+    lax.fori_loop(0, sources // 2, gather, 0, unroll=2)
 
     row = iota((AUX, HD), 0)
     for m in range(memories):
@@ -211,13 +220,12 @@
 
 def beside_kernel(
     cap,
-    in_hbm,
+    in_ref,
     kv_hbm,
     rate_ref,
     raw_hbm,
     faded_hbm,
     pick_hbm,
-    rows_ref,
     kv_ref,
     qg_ref,
     raw_ref,
@@ -225,7 +233,6 @@
     pick_ref,
     rates_ref,
     sums_ref,
-    rows_sem,
     kv_sem,
     pick_sem,
     raw_sem,
@@ -235,10 +242,6 @@
     pairs = pick_ref.shape[0]
     width = memories * 2 * cap
 
-    def rows_in(pair):
-        two = pl.ds(2 * pair, 2)
-        return pltpu.make_async_copy(in_hbm.at[two, 0:QA], rows_ref.at[two], rows_sem.at[pair])
-
     def kv_in(step):
         four = pl.ds(4 * step, 4)
         return pltpu.make_async_copy(kv_hbm.at[four], kv_ref.at[four], kv_sem.at[step])
@@ -253,8 +256,6 @@
             pltpu.make_async_copy(faded_ref.at[two], faded_hbm.at[two], faded_sem.at[step]),
         )
 
-    for pair in range(pairs):
-        rows_in(pair).start()
     for step in range(memories // 4):
         kv_in(step).start()
     head_rates(rate_ref, own_head(), rates_ref)
@@ -263,19 +264,18 @@
     sums_ref[TOK : 2 * TOK] = (tri < 0).astype(BF16)
     ones = jnp.ones((TOK, HD), BF16)
     eye = (tri == 0).astype(BF16)
-    down, across = iota((width, TOK), 0), iota((TOK, width), 1)
+    down, across = iota((width // 2, TOK), 0), iota((TOK, width), 1)
 
     def route(pair, carry):
-        rows_in(pair).wait()
         rows, select = [], []
         for side in range(2):
-            packed = rows_ref[2 * pair + side, TOK:QA]
+            packed = in_ref[2 * pair + side, TOK:QA]
             aux = packed.astype(F32)
             gamma = dot(jnp.where(tri == 0, aux[0:1], 0.0).astype(BF16), ones).astype(BF16)
-            rows.append(jnp.concatenate([rows_ref[2 * pair + side, 0:TOK], gamma], axis=1))
-            first, second = slot_ids(aux, cap, side)
+            rows.append(jnp.concatenate([in_ref[2 * pair + side, 0:TOK], gamma], axis=1))
+            first, second = own_slots(aux, cap)
             hit = (down == first) | (down == second)
-            select.append(jnp.where(hit, 1.0, 0.0).astype(BF16))
+            select.append(spread(jnp.where(hit, 1.0, 0.0), cap, side).astype(BF16))
             aux = nt(eye, packed)
             at = aux.astype(jnp.int32)
             first = at[:, 1:2] * (2 * cap) + at[:, 2:3] + side * cap
@@ -291,7 +291,7 @@
             qg_ref[m, at, :] = got[m * 2 * cap : (m + 1) * 2 * cap]
         return carry
 
-    lax.fori_loop(0, pairs, route, 0, unroll=1)
+    lax.fori_loop(0, pairs, route, 0)
     for step in range(memories // 4):
         kv_in(step).wait()
 
@@ -322,7 +322,7 @@
             copy.start()
         return carry
 
-    lax.fori_loop(0, memories // 2, intra, 0, unroll=1)
+    lax.fori_loop(0, memories // 2, intra, 0, unroll=2)
     for pair in range(pairs):
         pick_out(pair).wait()
     for step in range(memories // 2):
@@ -381,13 +381,18 @@
     return call(
         lambda *refs: pack_kernel(heads, *refs),
         like((heads, QA + 2 * TOK, HD), BF16),
-        [ANY, ANY, ANY, WHOLE, WHOLE, WHOLE],
+        [ANY] * 6,
         ANY,
         -2_000_000,
         (
+            pltpu.VMEM((heads, TOK), BF16),
+            pltpu.VMEM((2, TOK), jnp.int32),
+            pltpu.VMEM((2, TOK), F32),
+            pltpu.VMEM((3, TOK, heads * HD), BF16),
             pltpu.VMEM((heads, QA + 2 * TOK, HD), BF16),
-            DMA((3 * heads,)),
-            DMA((heads,)),
+            DMA((3,)),
+            DMA((3, GROUPS)),
+            DMA((GROUPS,)),
         ),
     )
 
@@ -401,19 +406,15 @@
             like((memories, slots, 2 * HD), BF16),
             like((parts, PART_ROWS + AUX, HD), BF16),
         ),
-        [ANY, WHOLE],
+        [WHOLE, WHOLE],
         (ANY, ANY),
-        -2_000_000,
+        ROOM,
         (
-            pltpu.VMEM((sources, AUX, TOK), BF16),
-            pltpu.VMEM((sources, 2 * TOK, HD), BF16),
             pltpu.VMEM((memories, slots, 2 * HD), BF16),
             pltpu.VMEM((memories, slots, HD), F32),
             pltpu.VMEM((parts, PART_ROWS + AUX, HD), BF16),
             pltpu.VMEM((memories, HD), F32),
             pltpu.VMEM((sources, memories, TOK), F32),
-            DMA((sources,)),
-            DMA(()),
             DMA((sources // 2,)),
             DMA((memories // 4,)),
         ),
@@ -440,11 +441,10 @@
     return call(
         lambda *refs: beside_kernel(cap, *refs),
         (like((memories, slots, HD), F32), like((memories, slots, HD), BF16), like(pick, BF16)),
-        [ANY, ANY, WHOLE],
+        [WHOLE, ANY, WHOLE],
         (ANY, ANY, ANY),
-        -2_000_000,
+        ROOM,
         (
-            pltpu.VMEM((sources, QA, HD), BF16),
             pltpu.VMEM((memories, slots, 2 * HD), BF16),
             pltpu.VMEM((memories, slots, 2 * HD), BF16),
             pltpu.VMEM((memories, slots, HD), F32),
@@ -452,7 +452,6 @@
             pltpu.VMEM(pick, BF16),
             pltpu.VMEM((memories, HD), F32),
             pltpu.VMEM((2 * TOK, TOK), BF16),
-            DMA((pairs,)),
             DMA((memories // 4,)),
             DMA((pairs,)),
             DMA((memories // 2,)),

time: 143 us -> 140 us (0.979)
  Pallas kernels: 32 us -> 28.7 us
    pallas_call x1, Pallas kernels: 8.59 us -> 4.66 us  [body(): slot_rows, update = gather(memories, sources, parts)(arrived, rate)]
  transfers between devices with their start and end apart: 1 -> 1, of which waited for: 1 -> 1; matrix products, arithmetic and copies ran while one was open for 0% -> 0% of each run, Pallas kernels for 11% -> 12%
where the time goes in v4:
time: 140 us; the launch traced here: 139 us
  blocking collectives  96.6 us (69%)
  Pallas kernels  28.7 us (20%)
  starting transfers between devices  11.1 us (8%)
  waiting for transfers between devices  2.87 us (2%)
    all_to_all x1, blocking collectives, body(): arrived = lax.all_to_all(send, 'mem', 0, 0, tiled=True)  51.9 us
    all_to_all x1, blocking collectives, body(): returned = lax.all_to_all(mixed, 'mem', 0, 0, tiled=True)  22.8 us
    all_to_all x1, blocking collectives, body(): lax.all_to_all(before, 'seq', 0, 0, tiled=True).reshape(memories, HD, HD)  21.9 us
    pallas_call x1, Pallas kernels, body(): raw, faded, pick = beside(memories, sources)(arrived, slot_rows, rate)  16.1 us
    all_to_all x1, starting transfers between devices, body(): pieces = lax.all_to_all(update, 'seq', 0, 0, tiled=True)  11.1 us
    pallas_call x1, Pallas kernels, body(): slot_rows, update = gather(memories, sources, parts)(arrived, rate)  4.66 us
    pallas_call x1, Pallas kernels, body(): mixed = finish(memories, sources)(faded, raw, pick, state, gain)  2.95 us
    all_to_all x1, waiting for transfers between devices, body(): pieces = lax.all_to_all(update, 'seq', 0, 0, tiled=True)  2.87 us
  transfers between devices with their start and end apart: 1, of which 1 were waited for; matrix products, arithmetic and copies ran while one was open for 0% of the time, Pallas kernels for 12%

profile of v4, /device:TPU:1, one launch (start us, length us, event | category | flops | bytes accessed | tf_op | source)
XLA Modules:
  0.0 139.4 jit_solution(17672062271454081354)
XLA Ops:
  0.0 0.0 copy-start.3
  0.0 2.7 %shard_map.82 = bf16[16,400,128]{2,1,0:T(8,128)(2,1)} custom-call(bf16[128,2048]{1,0:T(8,128)(2,1)} %refs_0_.1, bf16[128,2048]{1,0:T(8,128)(2,1)} %refs_1_.2, bf16[128,2048]{1,0:T(8,128)(2,1)} %refs_2_.2, bf16[16,128]{1,0:T(8,128)(2,1)} %bitcast.7, s32[2,128]{1,0:T(2,128)} %bitcast.8, f32[2,128]{1,0:T(2,128)} %bitcast.9), custom_call_target="tpu_custom_call" | custom-call | tf_op jit(solution)/shard_map/pallas_call | solution.py:487
  2.7 51.9 %all_to_all.20.refs_0_ = bf16[16,400,128]{2,1,0:T(8,128)(2,1)S(1)} all-to-all(bf16[16,400,128]{2,1,0:T(8,128)(2,1)} %shard_map.82), channel_id=1, replica_groups=mesh['seq'=32,'mem'=16] {'mem'}, dimensions={0} | all-to-all | bytes 3276800 | tf_op jit(solution)/shard_map/all_to_all | solution.py:488
  54.6 0.0 copy-done.3
  54.6 4.7 %shard_map.83 = (bf16[16,384,256]{2,1,0:T(8,128)(2,1)}, bf16[32,80,128]{2,1,0:T(8,128)(2,1)}) custom-call(bf16[16,400,128]{2,1,0:T(8,128)(2,1)S(1)} %all_to_all.20.refs_0_, bf16[16,16]{1,0:T(8,128)(2,1)S(1)} %copy-done.3), custom_call_target="tpu_custom_call" | custom-call | tf_op jit(solution)/shard_map/pallas_call | solution.py:489
  59.3 11.1 %all-to-all-start.1 = ((bf16[32,80,128]{2,1,0:T(8,128)(2,1)}), bf16[32,80,128]{2,1,0:T(8,128)(2,1)}, u32[]{:S(2)}, u32[]{:S(2)}) async-start(bf16[32,80,128]{2,1,0:T(8,128)(2,1)} %get-tuple-element.14), calls=%async_computation.1 | async-start | bytes 1310720 | tf_op jit(solution)/shard_map/all_to_all | solution.py:490
  70.4 16.1 %shard_map.84 = (f32[16,384,128]{2,1,0:T(8,128)}, bf16[16,384,128]{2,1,0:T(8,128)(2,1)S(1)}, bf16[8,256,768]{2,1,0:T(8,128)(2,1)}) custom-call(bf16[16,400,128]{2,1,0:T(8,128)(2,1)S(1)} %all_to_all.20.refs_0_, bf16[16,384,256]{2,1,0:T(8,128)(2,1)} %get-tuple-element.15.refs_1_, bf16[16,16]{1,0:T(8,128)(2,1)S(1)} %copy-done.3), custom_call_target="tpu_custom_call" | custom-call | flops 15000000512 | bytes 12582912 | tf_op jit(solution)/shard_map/pallas_call | solution.py:491
  86.5 2.9 %all-to-all-done.1.in_ref = bf16[32,80,128]{2,1,0:T(8,128)(2,1)} async-done(((bf16[32,80,128]{2,1,0:T(8,128)(2,1)}), bf16[32,80,128]{2,1,0:T(8,128)(2,1)}, u32[]{:S(2)}, u32[]{:S(2)}) %all-to-all-start.1) | async-done | bytes 655392 | tf_op jit(solution)/shard_map/all_to_all | solution.py:490
  89.4 0.0 copy-start
  89.4 0.0 copy-start.1
  89.4 0.0 copy-start.2
  89.4 1.4 shard_map.85
  90.8 21.9 %all_to_all.21 = bf16[32,64,128]{2,1,0:T(8,128)(2,1)S(1)} all-to-all(bf16[32,64,128]{2,1,0:T(8,128)(2,1)S(1)} %shard_map.85), channel_id=1, replica_groups=mesh['seq'=32,'mem'=16] {'seq'}, dimensions={0} | all-to-all | bytes 1048576 | tf_op jit(solution)/shard_map/all_to_all | solution.py:494
  112.7 0.0 copy-done
  112.7 0.0 copy-done.1
  112.7 0.0 copy-done.2
  112.7 2.9 %shard_map.86 = bf16[16,128,128]{2,1,0:T(8,128)(2,1)S(1)} custom-call(bf16[16,384,128]{2,1,0:T(8,128)(2,1)S(1)} %get-tuple-element.19.refs_0_, f32[16,384,128]{2,1,0:T(8,128)S(1)} %copy-done, bf16[8,256,768]{2,1,0:T(8,128)(2,1)S(1)} %copy-done.1, bf16[16,128,128]{2,1,0:T(8,128)(2,1)S(1)} %bitcast.5, f32[16,128]{1,0:T(8,128)S(1)} %bitcast.6), custom_call_target="tpu_custom_call" | custom-call | tf_op jit(solution)/shard_map/pallas_call | solution.py:496
  115.7 22.8 %all_to_all.22.in_ref = bf16[16,128,128]{2,1,0:T(8,128)(2,1)S(1)} all-to-all(bf16[16,128,128]{2,1,0:T(8,128)(2,1)S(1)} %shard_map.86), channel_id=1, replica_groups=mesh['seq'=32,'mem'=16] {'mem'}, dimensions={0} | all-to-all | bytes 1048576 | tf_op jit(solution)/shard_map/all_to_all | solution.py:497
  138.5 0.9 shard_map.87
Async XLA Ops:
  0.0 54.6 %copy-start.3 = (bf16[16,16]{1,0:T(8,128)(2,1)S(1)}, bf16[16,16]{1,0:T(8,128)(2,1)}, u32[]{:S(2)}) copy-start(bf16[16,16]{1,0:T(8,128)(2,1)} %refs_2_.3) | copy-start | bytes 1540
  59.3 30.1 %all-to-all-start.1 = ((bf16[32,80,128]{2,1,0:T(8,128)(2,1)}), bf16[32,80,128]{2,1,0:T(8,128)(2,1)}, u32[]{:S(2)}, u32[]{:S(2)}) async-start(bf16[32,80,128]{2,1,0:T(8,128)(2,1)} %get-tuple-element.14), calls=%async_computation.1 | async-start | bytes 1310720 | tf_op jit(solution)/shard_map/all_to_all | solution.py:490
  89.4 23.3 %copy-start = (f32[16,384,128]{2,1,0:T(8,128)S(1)}, f32[16,384,128]{2,1,0:T(8,128)}, u32[]{:S(2)}) copy-start(f32[16,384,128]{2,1,0:T(8,128)} %get-tuple-element.20.refs_1_) | copy-start | bytes 9437188
  89.4 23.3 %copy-start.1 = (bf16[8,256,768]{2,1,0:T(8,128)(2,1)S(1)}, bf16[8,256,768]{2,1,0:T(8,128)(2,1)}, u32[]{:S(2)}) copy-start(bf16[8,256,768]{2,1,0:T(8,128)(2,1)} %get-tuple-element.21.refs_2_) | copy-start | bytes 9437188
  89.4 23.3 %copy-start.2 = (f32[2048]{0:T(1024)S(1)}, f32[2048]{0:T(1024)}, u32[]{:S(2)}) copy-start(f32[2048]{0:T(1024)} %param.15) | copy-start | bytes 24580

commit v5 on v4

--- a/solution.py
+++ b/solution.py
@@ -14,7 +14,7 @@
 GROUPS = 2
 EPS = 1e-6
 VMEM_ALL = 58_000_000
-ROOM = 4_900_000
+ROOM = 4_200_000
 
 
 def iota(shape, dim):
@@ -224,13 +224,11 @@
     kv_hbm,
     rate_ref,
     raw_hbm,
-    faded_hbm,
-    pick_hbm,
+    rest_hbm,
     kv_ref,
     qg_ref,
     raw_ref,
-    faded_ref,
-    pick_ref,
+    rest_ref,
     rates_ref,
     sums_ref,
     kv_sem,
@@ -239,21 +237,23 @@
     faded_sem,
 ):
     memories, slots, _ = kv_ref.shape
-    pairs = pick_ref.shape[0]
+    pairs = in_ref.shape[0] // 2
     width = memories * 2 * cap
+    each = width // slots
 
     def kv_in(step):
         four = pl.ds(4 * step, 4)
         return pltpu.make_async_copy(kv_hbm.at[four], kv_ref.at[four], kv_sem.at[step])
 
     def pick_out(pair):
-        return pltpu.make_async_copy(pick_ref.at[pair], pick_hbm.at[pair], pick_sem.at[pair])
+        at = pl.ds(memories + each * pair, each)
+        return pltpu.make_async_copy(rest_ref.at[at], rest_hbm.at[at], pick_sem.at[pair])
 
     def made_out(step):
         two = pl.ds(2 * step, 2)
         return (
             pltpu.make_async_copy(raw_ref.at[two], raw_hbm.at[two], raw_sem.at[step]),
-            pltpu.make_async_copy(faded_ref.at[two], faded_hbm.at[two], faded_sem.at[step]),
+            pltpu.make_async_copy(rest_ref.at[two], rest_hbm.at[two], faded_sem.at[step]),
         )
 
     for step in range(memories // 4):
@@ -267,7 +267,7 @@
     down, across = iota((width // 2, TOK), 0), iota((TOK, width), 1)
 
     def route(pair, carry):
-        rows, select = [], []
+        rows, select, pick = [], [], jnp.zeros((TOK, width), F32)
         for side in range(2):
             packed = in_ref[2 * pair + side, TOK:QA]
             aux = packed.astype(F32)
@@ -282,8 +282,12 @@
             second = at[:, 3:4] * (2 * cap) + at[:, 4:5] + side * cap
             w0 = aux[:, 5:6] + aux[:, 7:8] + aux[:, 9:10]
             w1 = aux[:, 6:7] + aux[:, 8:9] + aux[:, 10:11]
-            pick = jnp.where(across == first, w0, jnp.where(across == second, w1, 0.0))
-            pick_ref[pair, side * TOK : (side + 1) * TOK] = pick.astype(BF16)
+            pick = jnp.where(across == first, w0, jnp.where(across == second, w1, pick))
+        for square in range(width // TOK):
+            which, row = divmod(square * TOK, slots)
+            lanes = slice(square * TOK, (square + 1) * TOK)
+            at = memories + each * pair + which
+            rest_ref[at, row : row + TOK] = pick[:, lanes].astype(BF16)
         pick_out(pair).start()
         got = dot(jnp.concatenate(select, axis=1), jnp.concatenate(rows, axis=0)).astype(BF16)
         at = pl.ds(pl.multiple_of(pair * 2 * cap, 2 * cap), 2 * cap)
@@ -300,6 +304,8 @@
             rate = rates_ref[pl.ds(m, 1), :]
             behind = []
             faded_all = jnp.ones((1, HD), F32)
+            scores = nt(qg_ref[m, :, 0:HD], kv_ref[m, :, 0:HD])
+            table = []
             for b in range(slots // TOK):
                 at = slice(b * TOK, (b + 1) * TOK)
                 seen = slice(0, (b + 1) * TOK)
@@ -309,15 +315,18 @@
                 sums = dot(sums_ref[...], jnp.concatenate([masked, gamma], axis=1))
                 inside = jnp.where(tri >= 0, jnp.exp(-rate * sums[0:TOK, 0:TOK]), 0.0)
                 fade = jnp.exp(-rate * sums[0:TOK, TOK : 2 * TOK])
-                faded_ref[m, at] = (q.astype(F32) * (fade * faded_all)).astype(BF16)
+                rest_ref[m, at] = (q.astype(F32) * (fade * faded_all)).astype(BF16)
                 decay = jnp.concatenate([fade * row for row in behind] + [inside], axis=1)
-                weights = (decay * nt(q, kv_ref[m, seen, 0:HD])).astype(BF16)
-                raw_ref[m, at] = dot(weights, kv_ref[m, seen, HD : 2 * HD])
+                weights = (decay * scores[at, seen]).astype(BF16)
                 if (b + 1) * TOK < slots:
+                    zeros = jnp.zeros((TOK, slots - (b + 1) * TOK), BF16)
+                    weights = jnp.concatenate([weights, zeros], axis=1)
                     whole = fade[TOK - 1 : TOK]
                     faded_all = faded_all * whole
                     rest = jnp.exp(-rate * sums[TOK : 2 * TOK, TOK : 2 * TOK])
                     behind = [row * whole for row in behind] + [rest.T]
+                table.append(weights)
+            raw_ref[m] = dot(jnp.concatenate(table, axis=0), kv_ref[m, :, HD : 2 * HD])
         for copy in made_out(step):
             copy.start()
         return carry
@@ -330,27 +339,37 @@
             copy.wait()
 
 
-def finish_kernel(cap, faded_ref, raw_ref, pick_ref, state_ref, gain_ref, out_ref, made_ref):
-    memories = faded_ref.shape[0]
+def finish_kernel(cap, rest_ref, raw_ref, state_ref, gain_ref, out_ref, made_ref):
+    memories, slots, _ = raw_ref.shape
+    width = memories * 2 * cap
+    each = width // slots
+    even = iota((slots, HD), 0) % (2 * cap) < cap
 
     def one(m, carry):
-        raw = raw_ref[m] + dot(faded_ref[m], state_ref[m])
+        raw = raw_ref[m] + dot(rest_ref[m], state_ref[m])
         mean = jnp.mean(raw * raw, axis=1, keepdims=True)
-        made_ref[m] = (raw * lax.rsqrt(mean + EPS)).astype(BF16)
+        made = raw * lax.rsqrt(mean + EPS)
+        made_ref[m, :, 0:HD] = jnp.where(even, made, 0.0).astype(BF16)
+        made_ref[m, :, HD : 2 * HD] = jnp.where(even, 0.0, made).astype(BF16)
         return carry
 
-    lax.fori_loop(0, memories, one, 0, unroll=4)
+    lax.fori_loop(0, memories, one, 0, unroll=8)
     gain = gain_ref[pl.ds(own_head(), 1), :]
 
     def mix(pair, carry):
         at = pl.ds(pl.multiple_of(pair * 2 * cap, 2 * cap), 2 * cap)
         rows = jnp.concatenate([made_ref[m, at, :] for m in range(memories)], axis=0)
-        mixed = (gain * dot(pick_ref[pair], rows)).astype(BF16)
+        squares = []
+        for square in range(width // TOK):
+            which, row = divmod(square * TOK, slots)
+            squares.append(rest_ref[memories + each * pair + which, row : row + TOK])
+        mixed = dot(jnp.concatenate(squares, axis=1), rows)
         for side in range(2):
-            out_ref[2 * pair + side] = mixed[side * TOK : (side + 1) * TOK]
+            own = mixed[:, side * HD : (side + 1) * HD]
+            out_ref[2 * pair + side] = (gain * own).astype(BF16)
         return carry
 
-    lax.fori_loop(0, pick_ref.shape[0], mix, 0, unroll=4)
+    lax.fori_loop(0, out_ref.shape[0] // 2, mix, 0, unroll=8)
 
 
 def unpack_kernel(in_ref, out_ref):
@@ -437,19 +456,18 @@
     cap = 3 * TOK // memories
     slots = sources * cap
     pairs = sources // 2
-    pick = (pairs, 2 * TOK, memories * 2 * cap)
+    rest = (memories + pairs * memories * 2 * cap // slots, slots, HD)
     return call(
         lambda *refs: beside_kernel(cap, *refs),
-        (like((memories, slots, HD), F32), like((memories, slots, HD), BF16), like(pick, BF16)),
+        (like((memories, slots, HD), F32), like(rest, BF16)),
         [WHOLE, ANY, WHOLE],
-        (ANY, ANY, ANY),
+        (ANY, ANY),
         ROOM,
         (
             pltpu.VMEM((memories, slots, 2 * HD), BF16),
             pltpu.VMEM((memories, slots, 2 * HD), BF16),
             pltpu.VMEM((memories, slots, HD), F32),
-            pltpu.VMEM((memories, slots, HD), BF16),
-            pltpu.VMEM(pick, BF16),
+            pltpu.VMEM(rest, BF16),
             pltpu.VMEM((memories, HD), F32),
             pltpu.VMEM((2 * TOK, TOK), BF16),
             DMA((memories // 4,)),
@@ -468,10 +486,10 @@
     return call(
         lambda *refs: finish_kernel(cap, *refs),
         like((sources, TOK, HD), BF16),
-        [WHOLE] * 5,
+        [WHOLE] * 4,
         WHOLE,
         40_000_000,
-        (pltpu.VMEM((memories, slots, HD), BF16),),
+        (pltpu.VMEM((memories, slots, 2 * HD), BF16),),
     )
 
 
@@ -488,12 +506,12 @@
     arrived = lax.all_to_all(send, "mem", 0, 0, tiled=True)
     slot_rows, update = gather(memories, sources, parts)(arrived, rate)
     pieces = lax.all_to_all(update, "seq", 0, 0, tiled=True)
-    raw, faded, pick = beside(memories, sources)(arrived, slot_rows, rate)
-    pieces, raw, faded, pick = lax.optimization_barrier((pieces, raw, faded, pick))
+    raw, rest = beside(memories, sources)(arrived, slot_rows, rate)
+    pieces, raw, rest = lax.optimization_barrier((pieces, raw, rest))
     before = scan(parts)(pieces)
     state = lax.all_to_all(before, "seq", 0, 0, tiled=True).reshape(memories, HD, HD)
     gain = norm_gain.reshape(heads, HD)
-    mixed = finish(memories, sources)(faded, raw, pick, state, gain)
+    mixed = finish(memories, sources)(rest, raw, state, gain)
     returned = lax.all_to_all(mixed, "mem", 0, 0, tiled=True)
     return unpack(heads)(returned)
 

time: 140 us -> 137 us (0.979)
  Pallas kernels: 28.7 us -> 22.8 us
  waiting for transfers between devices: 2.87 us -> 7.02 us
    pallas_call x2, Pallas kernels: 19.1 us -> 14.3 us  [the longest x1 12 us: body(): raw, rest = beside(memories, sources)(arrived, slot_rows, rate)]
    all_to_all x1, waiting for transfers between devices: 2.87 us -> 7.02 us  [body(): pieces = lax.all_to_all(update, 'seq', 0, 0, tiled=True)]
  transfers between devices with their start and end apart: 1 -> 1, of which waited for: 1 -> 1; matrix products, arithmetic and copies ran while one was open for 0% -> 0% of each run, Pallas kernels for 12% -> 9%
where the time goes in v5:
time: 137 us
  blocking collectives  96 us (70%)
  Pallas kernels  22.8 us (17%)
  starting transfers between devices  11 us (8%)
  waiting for transfers between devices  7.02 us (5%)
    all_to_all x1, blocking collectives, body(): arrived = lax.all_to_all(send, 'mem', 0, 0, tiled=True)  51.9 us
    all_to_all x1, blocking collectives, body(): returned = lax.all_to_all(mixed, 'mem', 0, 0, tiled=True)  23.4 us
    all_to_all x1, blocking collectives, body(): lax.all_to_all(before, 'seq', 0, 0, tiled=True).reshape(memories, HD, HD)  20.7 us
    pallas_call x1, Pallas kernels, body(): raw, rest = beside(memories, sources)(arrived, slot_rows, rate)  12 us
    all_to_all x1, starting transfers between devices, body(): pieces = lax.all_to_all(update, 'seq', 0, 0, tiled=True)  11 us
    all_to_all x1, waiting for transfers between devices, body(): pieces = lax.all_to_all(update, 'seq', 0, 0, tiled=True)  7.02 us
    pallas_call x1, Pallas kernels, body(): slot_rows, update = gather(memories, sources, parts)(arrived, rate)  4.67 us
  transfers between devices with their start and end apart: 1, of which 1 were waited for; matrix products, arithmetic and copies ran while one was open for 0% of the time, Pallas kernels for 9%

profile of v5, /device:TPU:1, one launch (start us, length us, event | category | flops | bytes accessed | tf_op | source)
XLA Modules:
  0.0 136.9 jit_solution(1871023770474847680)
XLA Ops:
  0.0 0.0 copy-start.3
  0.0 2.7 %shard_map.82 = bf16[16,400,128]{2,1,0:T(8,128)(2,1)} custom-call(bf16[128,2048]{1,0:T(8,128)(2,1)} %refs_0_.1, bf16[128,2048]{1,0:T(8,128)(2,1)} %refs_1_.2, bf16[128,2048]{1,0:T(8,128)(2,1)} %refs_2_.2, bf16[16,128]{1,0:T(8,128)(2,1)} %bitcast.7, s32[2,128]{1,0:T(2,128)} %bitcast.8, f32[2,128]{1,0:T(2,128)} %bitcast.9), custom_call_target="tpu_custom_call" | custom-call | tf_op jit(solution)/shard_map/pallas_call | solution.py:505
  2.7 51.9 %all_to_all.20.refs_0_ = bf16[16,400,128]{2,1,0:T(8,128)(2,1)S(1)} all-to-all(bf16[16,400,128]{2,1,0:T(8,128)(2,1)} %shard_map.82), channel_id=1, replica_groups=mesh['seq'=32,'mem'=16] {'mem'}, dimensions={0} | all-to-all | bytes 3276800 | tf_op jit(solution)/shard_map/all_to_all | solution.py:506
  54.7 0.0 copy-done.3
  54.7 4.7 %shard_map.83 = (bf16[16,384,256]{2,1,0:T(8,128)(2,1)}, bf16[32,80,128]{2,1,0:T(8,128)(2,1)}) custom-call(bf16[16,400,128]{2,1,0:T(8,128)(2,1)S(1)} %all_to_all.20.refs_0_, bf16[16,16]{1,0:T(8,128)(2,1)S(1)} %copy-done.3), custom_call_target="tpu_custom_call" | custom-call | tf_op jit(solution)/shard_map/pallas_call | solution.py:507
  59.3 11.0 %all-to-all-start.1 = ((bf16[32,80,128]{2,1,0:T(8,128)(2,1)}), bf16[32,80,128]{2,1,0:T(8,128)(2,1)S(1)}, u32[]{:S(2)}, u32[]{:S(2)}) async-start(bf16[32,80,128]{2,1,0:T(8,128)(2,1)} %get-tuple-element.12), calls=%async_computation.1 | async-start | bytes 1310720 | tf_op jit(solution)/shard_map/all_to_all | solution.py:508
  70.3 12.0 %shard_map.84 = (f32[16,384,128]{2,1,0:T(8,128)}, bf16[32,384,128]{2,1,0:T(8,128)(2,1)}) custom-call(bf16[16,400,128]{2,1,0:T(8,128)(2,1)S(1)} %all_to_all.20.refs_0_, bf16[16,384,256]{2,1,0:T(8,128)(2,1)} %get-tuple-element.13.refs_1_, bf16[16,16]{1,0:T(8,128)(2,1)S(1)} %copy-done.3), custom_call_target="tpu_custom_call" | custom-call | flops 15000000512 | bytes 12582912 | tf_op jit(solution)/shard_map/pallas_call | solution.py:509
  82.3 7.0 %all-to-all-done.1.in_ref = bf16[32,80,128]{2,1,0:T(8,128)(2,1)S(1)} async-done(((bf16[32,80,128]{2,1,0:T(8,128)(2,1)}), bf16[32,80,128]{2,1,0:T(8,128)(2,1)S(1)}, u32[]{:S(2)}, u32[]{:S(2)}) %all-to-all-start.1) | async-done | bytes 655392 | tf_op jit(solution)/shard_map/all_to_all | solution.py:508
  89.3 0.0 copy-start
  89.4 0.0 copy-start.1
  89.4 0.0 copy-start.2
  89.4 0.2 shard_map.85
  89.5 20.7 %all_to_all.21 = bf16[32,64,128]{2,1,0:T(8,128)(2,1)S(1)} all-to-all(bf16[32,64,128]{2,1,0:T(8,128)(2,1)S(1)} %shard_map.85), channel_id=1, replica_groups=mesh['seq'=32,'mem'=16] {'seq'}, dimensions={0} | all-to-all | bytes 1048576 | tf_op jit(solution)/shard_map/all_to_all | solution.py:512
  110.2 0.0 copy-done
  110.2 0.0 copy-done.1
  110.2 0.0 copy-done.2
  110.2 2.4 %shard_map.86 = bf16[16,128,128]{2,1,0:T(8,128)(2,1)S(1)} custom-call(bf16[32,384,128]{2,1,0:T(8,128)(2,1)S(1)} %copy-done.1, f32[16,384,128]{2,1,0:T(8,128)S(1)} %copy-done, bf16[16,128,128]{2,1,0:T(8,128)(2,1)S(1)} %bitcast.5, f32[16,128]{1,0:T(8,128)S(1)} %bitcast.6), custom_call_target="tpu_custom_call" | custom-call | tf_op jit(solution)/shard_map/pallas_call | solution.py:514
  112.6 23.4 %all_to_all.22.in_ref = bf16[16,128,128]{2,1,0:T(8,128)(2,1)S(1)} all-to-all(bf16[16,128,128]{2,1,0:T(8,128)(2,1)S(1)} %shard_map.86), channel_id=1, replica_groups=mesh['seq'=32,'mem'=16] {'mem'}, dimensions={0} | all-to-all | bytes 1048576 | tf_op jit(solution)/shard_map/all_to_all | solution.py:515
  136.0 0.9 shard_map.87
Async XLA Ops:
  0.0 54.7 %copy-start.3 = (bf16[16,16]{1,0:T(8,128)(2,1)S(1)}, bf16[16,16]{1,0:T(8,128)(2,1)}, u32[]{:S(2)}) copy-start(bf16[16,16]{1,0:T(8,128)(2,1)} %refs_2_.3) | copy-start | bytes 1540
  59.3 30.0 %all-to-all-start.1 = ((bf16[32,80,128]{2,1,0:T(8,128)(2,1)}), bf16[32,80,128]{2,1,0:T(8,128)(2,1)S(1)}, u32[]{:S(2)}, u32[]{:S(2)}) async-start(bf16[32,80,128]{2,1,0:T(8,128)(2,1)} %get-tuple-element.12), calls=%async_computation.1 | async-start | bytes 1310720 | tf_op jit(solution)/shard_map/all_to_all | solution.py:508
  89.3 20.9 %copy-start = (f32[16,384,128]{2,1,0:T(8,128)S(1)}, f32[16,384,128]{2,1,0:T(8,128)}, u32[]{:S(2)}) copy-start(f32[16,384,128]{2,1,0:T(8,128)} %get-tuple-element.17.refs_1_) | copy-start | bytes 9437188
  89.4 20.9 %copy-start.1 = (bf16[32,384,128]{2,1,0:T(8,128)(2,1)S(1)}, bf16[32,384,128]{2,1,0:T(8,128)(2,1)}, u32[]{:S(2)}) copy-start(bf16[32,384,128]{2,1,0:T(8,128)(2,1)} %get-tuple-element.16.refs_0_) | copy-start | bytes 9437188
  89.4 20.9 %copy-start.2 = (f32[2048]{0:T(1024)S(1)}, f32[2048]{0:T(1024)}, u32[]{:S(2)}) copy-start(f32[2048]{0:T(1024)} %param.15) | copy-start | bytes 24580

commit v6 on v5

--- a/solution.py
+++ b/solution.py
@@ -175,7 +175,7 @@
         at = pl.ds(pl.multiple_of(pair * 2 * cap, 2 * cap), 2 * cap)
         return pltpu.make_async_copy(slots_ref.at[:, at], slots_out.at[:, at], slots_sem.at[pair])
 
-    lax.fori_loop(0, sources // 2, gather, 0, unroll=2)
+    lax.fori_loop(0, sources // 2, gather, 0, unroll=4)
 
     row = iota((AUX, HD), 0)
     for m in range(memories):
@@ -202,7 +202,7 @@
         updated(step).start()
         return carry
 
-    lax.fori_loop(0, memories // 4, update, 0)
+    lax.fori_loop(0, memories // 4, update, 0, unroll=4)
     for step in range(memories // 4):
         updated(step).wait()
     for pair in range(sources // 2):
@@ -353,7 +353,7 @@
         made_ref[m, :, HD : 2 * HD] = jnp.where(even, 0.0, made).astype(BF16)
         return carry
 
-    lax.fori_loop(0, memories, one, 0, unroll=8)
+    lax.fori_loop(0, memories, one, 0, unroll=16)
     gain = gain_ref[pl.ds(own_head(), 1), :]
 
     def mix(pair, carry):

time: 137 us -> 136 us (level)
  no operation moved by 1% of the time
where the time goes in v6:
time: 136 us
  blocking collectives  96 us (71%)
  Pallas kernels  21.6 us (16%)
  starting transfers between devices  11 us (8%)
  waiting for transfers between devices  7.02 us (5%)
    all_to_all x1, blocking collectives, body(): arrived = lax.all_to_all(send, 'mem', 0, 0, tiled=True)  51.9 us
    all_to_all x1, blocking collectives, body(): returned = lax.all_to_all(mixed, 'mem', 0, 0, tiled=True)  23.4 us
    all_to_all x1, blocking collectives, body(): lax.all_to_all(before, 'seq', 0, 0, tiled=True).reshape(memories, HD, HD)  20.7 us
    pallas_call x1, Pallas kernels, body(): raw, rest = beside(memories, sources)(arrived, slot_rows, rate)  12 us
    all_to_all x1, starting transfers between devices, body(): pieces = lax.all_to_all(update, 'seq', 0, 0, tiled=True)  11 us
    all_to_all x1, waiting for transfers between devices, body(): pieces = lax.all_to_all(update, 'seq', 0, 0, tiled=True)  7.02 us
    pallas_call x1, Pallas kernels, body(): slot_rows, update = gather(memories, sources, parts)(arrived, rate)  3.87 us
  transfers between devices with their start and end apart: 1, of which 1 were waited for; matrix products, arithmetic and copies ran while one was open for 0% of the time, Pallas kernels for 9%

profile of v6, /device:TPU:1, one launch (start us, length us, event | category | flops | bytes accessed | tf_op | source)
XLA Modules:
  0.0 135.7 jit_solution(6982640463521269200)
XLA Ops:
  0.0 0.0 copy-start.3
  0.0 2.7 %shard_map.82 = bf16[16,400,128]{2,1,0:T(8,128)(2,1)} custom-call(bf16[128,2048]{1,0:T(8,128)(2,1)} %refs_0_.1, bf16[128,2048]{1,0:T(8,128)(2,1)} %refs_1_.2, bf16[128,2048]{1,0:T(8,128)(2,1)} %refs_2_.2, bf16[16,128]{1,0:T(8,128)(2,1)} %bitcast.7, s32[2,128]{1,0:T(2,128)} %bitcast.8, f32[2,128]{1,0:T(2,128)} %bitcast.9), custom_call_target="tpu_custom_call" | custom-call | tf_op jit(solution)/shard_map/pallas_call | solution.py:505
  2.7 51.9 %all_to_all.20.refs_0_ = bf16[16,400,128]{2,1,0:T(8,128)(2,1)S(1)} all-to-all(bf16[16,400,128]{2,1,0:T(8,128)(2,1)} %shard_map.82), channel_id=1, replica_groups=mesh['seq'=32,'mem'=16] {'mem'}, dimensions={0} | all-to-all | bytes 3276800 | tf_op jit(solution)/shard_map/all_to_all | solution.py:506
  54.7 0.0 copy-done.3
  54.7 3.9 %shard_map.83 = (bf16[16,384,256]{2,1,0:T(8,128)(2,1)}, bf16[32,80,128]{2,1,0:T(8,128)(2,1)}) custom-call(bf16[16,400,128]{2,1,0:T(8,128)(2,1)S(1)} %all_to_all.20.refs_0_, bf16[16,16]{1,0:T(8,128)(2,1)S(1)} %copy-done.3), custom_call_target="tpu_custom_call" | custom-call | tf_op jit(solution)/shard_map/pallas_call | solution.py:507
  58.5 11.0 %all-to-all-start.1 = ((bf16[32,80,128]{2,1,0:T(8,128)(2,1)}), bf16[32,80,128]{2,1,0:T(8,128)(2,1)S(1)}, u32[]{:S(2)}, u32[]{:S(2)}) async-start(bf16[32,80,128]{2,1,0:T(8,128)(2,1)} %get-tuple-element.12), calls=%async_computation.1 | async-start | bytes 1310720 | tf_op jit(solution)/shard_map/all_to_all | solution.py:508
  69.5 12.0 %shard_map.84 = (f32[16,384,128]{2,1,0:T(8,128)}, bf16[32,384,128]{2,1,0:T(8,128)(2,1)}) custom-call(bf16[16,400,128]{2,1,0:T(8,128)(2,1)S(1)} %all_to_all.20.refs_0_, bf16[16,384,256]{2,1,0:T(8,128)(2,1)} %get-tuple-element.13.refs_1_, bf16[16,16]{1,0:T(8,128)(2,1)S(1)} %copy-done.3), custom_call_target="tpu_custom_call" | custom-call | flops 15000000512 | bytes 12582912 | tf_op jit(solution)/shard_map/pallas_call | solution.py:509
  81.5 7.0 %all-to-all-done.1.in_ref = bf16[32,80,128]{2,1,0:T(8,128)(2,1)S(1)} async-done(((bf16[32,80,128]{2,1,0:T(8,128)(2,1)}), bf16[32,80,128]{2,1,0:T(8,128)(2,1)S(1)}, u32[]{:S(2)}, u32[]{:S(2)}) %all-to-all-start.1) | async-done | bytes 655392 | tf_op jit(solution)/shard_map/all_to_all | solution.py:508
  88.5 0.0 copy-start
  88.6 0.0 copy-start.1
  88.6 0.0 copy-start.2
  88.6 0.2 shard_map.85
  88.7 20.7 %all_to_all.21 = bf16[32,64,128]{2,1,0:T(8,128)(2,1)S(1)} all-to-all(bf16[32,64,128]{2,1,0:T(8,128)(2,1)S(1)} %shard_map.85), channel_id=1, replica_groups=mesh['seq'=32,'mem'=16] {'seq'}, dimensions={0} | all-to-all | bytes 1048576 | tf_op jit(solution)/shard_map/all_to_all | solution.py:512
  109.4 0.0 copy-done
  109.4 0.0 copy-done.1
  109.4 0.0 copy-done.2
  109.4 1.9 %shard_map.86 = bf16[16,128,128]{2,1,0:T(8,128)(2,1)S(1)} custom-call(bf16[32,384,128]{2,1,0:T(8,128)(2,1)S(1)} %copy-done.1, f32[16,384,128]{2,1,0:T(8,128)S(1)} %copy-done, bf16[16,128,128]{2,1,0:T(8,128)(2,1)S(1)} %bitcast.5, f32[16,128]{1,0:T(8,128)S(1)} %bitcast.6), custom_call_target="tpu_custom_call" | custom-call | tf_op jit(solution)/shard_map/pallas_call | solution.py:514
  111.4 23.4 %all_to_all.22.in_ref = bf16[16,128,128]{2,1,0:T(8,128)(2,1)S(1)} all-to-all(bf16[16,128,128]{2,1,0:T(8,128)(2,1)S(1)} %shard_map.86), channel_id=1, replica_groups=mesh['seq'=32,'mem'=16] {'mem'}, dimensions={0} | all-to-all | bytes 1048576 | tf_op jit(solution)/shard_map/all_to_all | solution.py:515
  134.8 0.9 shard_map.87
Async XLA Ops:
  0.0 54.7 %copy-start.3 = (bf16[16,16]{1,0:T(8,128)(2,1)S(1)}, bf16[16,16]{1,0:T(8,128)(2,1)}, u32[]{:S(2)}) copy-start(bf16[16,16]{1,0:T(8,128)(2,1)} %refs_2_.3) | copy-start | bytes 1540
  58.5 30.0 %all-to-all-start.1 = ((bf16[32,80,128]{2,1,0:T(8,128)(2,1)}), bf16[32,80,128]{2,1,0:T(8,128)(2,1)S(1)}, u32[]{:S(2)}, u32[]{:S(2)}) async-start(bf16[32,80,128]{2,1,0:T(8,128)(2,1)} %get-tuple-element.12), calls=%async_computation.1 | async-start | bytes 1310720 | tf_op jit(solution)/shard_map/all_to_all | solution.py:508
  88.5 20.9 %copy-start = (f32[16,384,128]{2,1,0:T(8,128)S(1)}, f32[16,384,128]{2,1,0:T(8,128)}, u32[]{:S(2)}) copy-start(f32[16,384,128]{2,1,0:T(8,128)} %get-tuple-element.17.refs_1_) | copy-start | bytes 9437188
  88.6 20.9 %copy-start.1 = (bf16[32,384,128]{2,1,0:T(8,128)(2,1)S(1)}, bf16[32,384,128]{2,1,0:T(8,128)(2,1)}, u32[]{:S(2)}) copy-start(bf16[32,384,128]{2,1,0:T(8,128)(2,1)} %get-tuple-element.16.refs_0_) | copy-start | bytes 9437188
  88.6 20.9 %copy-start.2 = (f32[2048]{0:T(1024)S(1)}, f32[2048]{0:T(1024)}, u32[]{:S(2)}) copy-start(f32[2048]{0:T(1024)} %param.15) | copy-start | bytes 24580

commit v7 on v6

--- a/solution.py
+++ b/solution.py
@@ -175,7 +175,7 @@
         at = pl.ds(pl.multiple_of(pair * 2 * cap, 2 * cap), 2 * cap)
         return pltpu.make_async_copy(slots_ref.at[:, at], slots_out.at[:, at], slots_sem.at[pair])
 
-    lax.fori_loop(0, sources // 2, gather, 0, unroll=4)
+    lax.fori_loop(0, sources // 2, gather, 0, unroll=8)
 
     row = iota((AUX, HD), 0)
     for m in range(memories):

time: 136 us -> 135 us (level)
  no operation moved by 1% of the time
where the time goes in v7:
time: 135 us
  blocking collectives  96 us (71%)
  Pallas kernels  21.1 us (16%)
  starting transfers between devices  11 us (8%)
  waiting for transfers between devices  7.02 us (5%)
    all_to_all x1, blocking collectives, body(): arrived = lax.all_to_all(send, 'mem', 0, 0, tiled=True)  51.9 us
    all_to_all x1, blocking collectives, body(): returned = lax.all_to_all(mixed, 'mem', 0, 0, tiled=True)  23.3 us
    all_to_all x1, blocking collectives, body(): lax.all_to_all(before, 'seq', 0, 0, tiled=True).reshape(memories, HD, HD)  20.8 us
    pallas_call x1, Pallas kernels, body(): raw, rest = beside(memories, sources)(arrived, slot_rows, rate)  12 us
    all_to_all x1, starting transfers between devices, body(): pieces = lax.all_to_all(update, 'seq', 0, 0, tiled=True)  11 us
    all_to_all x1, waiting for transfers between devices, body(): pieces = lax.all_to_all(update, 'seq', 0, 0, tiled=True)  7.02 us
    pallas_call x1, Pallas kernels, body(): slot_rows, update = gather(memories, sources, parts)(arrived, rate)  3.34 us
    pallas_call x1, Pallas kernels, body(): pack(heads)(queries, keys, values, gamma.T, route_ids.T, route_weights.T)  2.71 us
  transfers between devices with their start and end apart: 1, of which 1 were waited for; matrix products, arithmetic and copies ran while one was open for 0% of the time, Pallas kernels for 9%

profile of v7, /device:TPU:1, one launch (start us, length us, event | category | flops | bytes accessed | tf_op | source)
XLA Modules:
  0.0 135.2 jit_solution(3584733694736175018)
XLA Ops:
  0.0 0.0 copy-start.3
  0.0 2.7 %shard_map.82 = bf16[16,400,128]{2,1,0:T(8,128)(2,1)} custom-call(bf16[128,2048]{1,0:T(8,128)(2,1)} %refs_0_.1, bf16[128,2048]{1,0:T(8,128)(2,1)} %refs_1_.2, bf16[128,2048]{1,0:T(8,128)(2,1)} %refs_2_.2, bf16[16,128]{1,0:T(8,128)(2,1)} %bitcast.7, s32[2,128]{1,0:T(2,128)} %bitcast.8, f32[2,128]{1,0:T(2,128)} %bitcast.9), custom_call_target="tpu_custom_call" | custom-call | tf_op jit(solution)/shard_map/pallas_call | solution.py:505
  2.7 51.9 %all_to_all.20.refs_0_ = bf16[16,400,128]{2,1,0:T(8,128)(2,1)S(1)} all-to-all(bf16[16,400,128]{2,1,0:T(8,128)(2,1)} %shard_map.82), channel_id=1, replica_groups=mesh['seq'=32,'mem'=16] {'mem'}, dimensions={0} | all-to-all | bytes 3276800 | tf_op jit(solution)/shard_map/all_to_all | solution.py:506
  54.7 0.0 copy-done.3
  54.7 3.3 %shard_map.83 = (bf16[16,384,256]{2,1,0:T(8,128)(2,1)}, bf16[32,80,128]{2,1,0:T(8,128)(2,1)}) custom-call(bf16[16,400,128]{2,1,0:T(8,128)(2,1)S(1)} %all_to_all.20.refs_0_, bf16[16,16]{1,0:T(8,128)(2,1)S(1)} %copy-done.3), custom_call_target="tpu_custom_call" | custom-call | tf_op jit(solution)/shard_map/pallas_call | solution.py:507
  58.0 11.0 %all-to-all-start.1 = ((bf16[32,80,128]{2,1,0:T(8,128)(2,1)}), bf16[32,80,128]{2,1,0:T(8,128)(2,1)S(1)}, u32[]{:S(2)}, u32[]{:S(2)}) async-start(bf16[32,80,128]{2,1,0:T(8,128)(2,1)} %get-tuple-element.12), calls=%async_computation.1 | async-start | bytes 1310720 | tf_op jit(solution)/shard_map/all_to_all | solution.py:508
  69.0 12.0 %shard_map.84 = (f32[16,384,128]{2,1,0:T(8,128)}, bf16[32,384,128]{2,1,0:T(8,128)(2,1)}) custom-call(bf16[16,400,128]{2,1,0:T(8,128)(2,1)S(1)} %all_to_all.20.refs_0_, bf16[16,384,256]{2,1,0:T(8,128)(2,1)} %get-tuple-element.13.refs_1_, bf16[16,16]{1,0:T(8,128)(2,1)S(1)} %copy-done.3), custom_call_target="tpu_custom_call" | custom-call | flops 15000000512 | bytes 12582912 | tf_op jit(solution)/shard_map/pallas_call | solution.py:509
  81.0 7.0 %all-to-all-done.1.in_ref = bf16[32,80,128]{2,1,0:T(8,128)(2,1)S(1)} async-done(((bf16[32,80,128]{2,1,0:T(8,128)(2,1)}), bf16[32,80,128]{2,1,0:T(8,128)(2,1)S(1)}, u32[]{:S(2)}, u32[]{:S(2)}) %all-to-all-start.1) | async-done | bytes 655392 | tf_op jit(solution)/shard_map/all_to_all | solution.py:508
  88.0 0.0 copy-start
  88.0 0.0 copy-start.1
  88.0 0.0 copy-start.2
  88.0 0.2 shard_map.85
  88.2 20.8 %all_to_all.21 = bf16[32,64,128]{2,1,0:T(8,128)(2,1)S(1)} all-to-all(bf16[32,64,128]{2,1,0:T(8,128)(2,1)S(1)} %shard_map.85), channel_id=1, replica_groups=mesh['seq'=32,'mem'=16] {'seq'}, dimensions={0} | all-to-all | bytes 1048576 | tf_op jit(solution)/shard_map/all_to_all | solution.py:512
  108.9 0.0 copy-done
  108.9 0.0 copy-done.1
  108.9 0.0 copy-done.2
  108.9 2.0 %shard_map.86 = bf16[16,128,128]{2,1,0:T(8,128)(2,1)S(1)} custom-call(bf16[32,384,128]{2,1,0:T(8,128)(2,1)S(1)} %copy-done.1, f32[16,384,128]{2,1,0:T(8,128)S(1)} %copy-done, bf16[16,128,128]{2,1,0:T(8,128)(2,1)S(1)} %bitcast.5, f32[16,128]{1,0:T(8,128)S(1)} %bitcast.6), custom_call_target="tpu_custom_call" | custom-call | tf_op jit(solution)/shard_map/pallas_call | solution.py:514
  110.9 23.3 %all_to_all.22.in_ref = bf16[16,128,128]{2,1,0:T(8,128)(2,1)S(1)} all-to-all(bf16[16,128,128]{2,1,0:T(8,128)(2,1)S(1)} %shard_map.86), channel_id=1, replica_groups=mesh['seq'=32,'mem'=16] {'mem'}, dimensions={0} | all-to-all | bytes 1048576 | tf_op jit(solution)/shard_map/all_to_all | solution.py:515
  134.2 0.9 shard_map.87
Async XLA Ops:
  0.0 54.7 %copy-start.3 = (bf16[16,16]{1,0:T(8,128)(2,1)S(1)}, bf16[16,16]{1,0:T(8,128)(2,1)}, u32[]{:S(2)}) copy-start(bf16[16,16]{1,0:T(8,128)(2,1)} %refs_2_.3) | copy-start | bytes 1540
  58.0 30.0 %all-to-all-start.1 = ((bf16[32,80,128]{2,1,0:T(8,128)(2,1)}), bf16[32,80,128]{2,1,0:T(8,128)(2,1)S(1)}, u32[]{:S(2)}, u32[]{:S(2)}) async-start(bf16[32,80,128]{2,1,0:T(8,128)(2,1)} %get-tuple-element.12), calls=%async_computation.1 | async-start | bytes 1310720 | tf_op jit(solution)/shard_map/all_to_all | solution.py:508
  88.0 20.9 %copy-start = (f32[16,384,128]{2,1,0:T(8,128)S(1)}, f32[16,384,128]{2,1,0:T(8,128)}, u32[]{:S(2)}) copy-start(f32[16,384,128]{2,1,0:T(8,128)} %get-tuple-element.17.refs_1_) | copy-start | bytes 9437188
  88.0 20.9 %copy-start.1 = (bf16[32,384,128]{2,1,0:T(8,128)(2,1)S(1)}, bf16[32,384,128]{2,1,0:T(8,128)(2,1)}, u32[]{:S(2)}) copy-start(bf16[32,384,128]{2,1,0:T(8,128)(2,1)} %get-tuple-element.16.refs_0_) | copy-start | bytes 9437188
  88.0 20.9 %copy-start.2 = (f32[2048]{0:T(1024)S(1)}, f32[2048]{0:T(1024)}, u32[]{:S(2)}) copy-start(f32[2048]{0:T(1024)} %param.15) | copy-start | bytes 24580

commit v8 on v7

--- a/solution.py
+++ b/solution.py
@@ -46,7 +46,7 @@
 def pack_kernel(
     heads, q_ref, k_ref, v_ref, gamma_hbm, ids_hbm, weights_hbm, out_ref, gamma_ref, ids_ref, weights_ref, given_ref, rows_ref, small_sem, sem, out_sem
 ):
-    groups, lanes = out_sem.shape[0], heads * HD // out_sem.shape[0]
+    groups, lanes = GROUPS, heads * HD // GROUPS
 
     def arriving(group):
         at = slice(group * lanes, (group + 1) * lanes)
@@ -60,11 +60,25 @@
         pltpu.make_async_copy(ids_hbm, ids_ref, small_sem.at[1]),
         pltpu.make_async_copy(weights_hbm, weights_ref, small_sem.at[2]),
     ]
-    for copy in small:
-        copy.start()
     for group in range(groups):
         for copy in arriving(group):
             copy.start()
+    for copy in small:
+        copy.start()
+    leaving = []
+    for group in range(groups):
+        for copy in arriving(group):
+            copy.wait()
+        some = range(group * heads // groups, (group + 1) * heads // groups)
+        for h in some:
+            for which, at in enumerate((0, QA, QA + TOK)):
+                rows_ref[h, at : at + TOK] = given_ref[which, :, h * HD : (h + 1) * HD]
+        at = pl.ds(some[0], len(some))
+        for part, (low, high) in enumerate(((0, TOK), (QA, QA + 2 * TOK))):
+            rows = rows_ref.at[at, low:high]
+            copy = pltpu.make_async_copy(rows, out_ref.at[at, low:high], out_sem.at[part, group])
+            copy.start()
+            leaving.append(copy)
     for copy in small:
         copy.wait()
     ids = ids_ref[...]
@@ -87,17 +101,9 @@
     for h in range(heads):
         aux = jnp.where(row == 0, gamma_rows[h : h + 1], shared)
         rows_ref[h, TOK:QA] = aux.astype(BF16)
-    leaving = []
-    for group in range(groups):
-        for copy in arriving(group):
-            copy.wait()
-        some = range(group * heads // groups, (group + 1) * heads // groups)
-        for h in some:
-            for which, at in enumerate((0, QA, QA + TOK)):
-                rows_ref[h, at : at + TOK] = given_ref[which, :, h * HD : (h + 1) * HD]
-        at = pl.ds(some[0], len(some))
-        leaving.append(pltpu.make_async_copy(rows_ref.at[at], out_ref.at[at], out_sem.at[group]))
-        leaving[group].start()
+    small_rows = pltpu.make_async_copy(rows_ref.at[:, TOK:QA], out_ref.at[:, TOK:QA], out_sem.at[2, 0])
+    small_rows.start()
+    leaving.append(small_rows)
     for copy in leaving:
         copy.wait()
 
@@ -372,9 +378,18 @@
     lax.fori_loop(0, out_ref.shape[0] // 2, mix, 0, unroll=8)
 
 
-def unpack_kernel(in_ref, out_ref):
-    for h in range(in_ref.shape[0]):
-        out_ref[:, h * HD : (h + 1) * HD] = in_ref[h]
+def unpack_kernel(in_ref, out_ref, rows_ref, sem):
+    heads = in_ref.shape[0]
+    copies = []
+    for part in range(2):
+        some = range(part * heads // 2, (part + 1) * heads // 2)
+        for h in some:
+            rows_ref[:, h * HD : (h + 1) * HD] = in_ref[h]
+        at = slice(some[0] * HD, (some[-1] + 1) * HD)
+        copies.append(pltpu.make_async_copy(rows_ref.at[:, at], out_ref.at[:, at], sem.at[part]))
+        copies[part].start()
+    for copy in copies:
+        copy.wait()
 
 
 like = jax.ShapeDtypeStruct
@@ -411,7 +426,7 @@
             pltpu.VMEM((heads, QA + 2 * TOK, HD), BF16),
             DMA((3,)),
             DMA((3, GROUPS)),
-            DMA((GROUPS,)),
+            DMA((3, GROUPS)),
         ),
     )
 
@@ -494,7 +509,7 @@
 
 
 def unpack(heads):
-    return call(unpack_kernel, like((TOK, heads * HD), BF16), [WHOLE], WHOLE, 40_000_000)
+    return call(unpack_kernel, like((TOK, heads * HD), BF16), [WHOLE], ANY, 40_000_000, (pltpu.VMEM((TOK, heads * HD), BF16), DMA((2,))))
 
 
 def body(queries, keys, values, gamma, rate, route_ids, route_weights, norm_gain):

time: 135 us -> 135 us (level)
  no operation moved by 1% of the time
where the time goes in v8:
time: 135 us
  blocking collectives  96 us (71%)
  Pallas kernels  20.9 us (15%)
  starting transfers between devices  11 us (8%)
  waiting for transfers between devices  7.02 us (5%)
    all_to_all x1, blocking collectives, body(): arrived = lax.all_to_all(send, 'mem', 0, 0, tiled=True)  51.9 us
    all_to_all x1, blocking collectives, body(): returned = lax.all_to_all(mixed, 'mem', 0, 0, tiled=True)  23.4 us
    all_to_all x1, blocking collectives, body(): lax.all_to_all(before, 'seq', 0, 0, tiled=True).reshape(memories, HD, HD)  20.7 us
    pallas_call x1, Pallas kernels, body(): raw, rest = beside(memories, sources)(arrived, slot_rows, rate)  12 us
    all_to_all x1, starting transfers between devices, body(): pieces = lax.all_to_all(update, 'seq', 0, 0, tiled=True)  11 us
    all_to_all x1, waiting for transfers between devices, body(): pieces = lax.all_to_all(update, 'seq', 0, 0, tiled=True)  7.02 us
    pallas_call x1, Pallas kernels, body(): slot_rows, update = gather(memories, sources, parts)(arrived, rate)  3.34 us
  transfers between devices with their start and end apart: 1, of which 1 were waited for; matrix products, arithmetic and copies ran while one was open for 0% of the time, Pallas kernels for 9%

profile of v8, /device:TPU:1, one launch (start us, length us, event | category | flops | bytes accessed | tf_op | source)
XLA Modules:
  0.0 135.0 jit_solution(5487187376692922831)
XLA Ops:
  0.0 0.0 copy-start.3
  0.0 2.6 %shard_map.82 = bf16[16,400,128]{2,1,0:T(8,128)(2,1)} custom-call(bf16[128,2048]{1,0:T(8,128)(2,1)} %refs_0_.1, bf16[128,2048]{1,0:T(8,128)(2,1)} %refs_1_.2, bf16[128,2048]{1,0:T(8,128)(2,1)} %refs_2_.2, bf16[16,128]{1,0:T(8,128)(2,1)} %bitcast.7, s32[2,128]{1,0:T(2,128)} %bitcast.8, f32[2,128]{1,0:T(2,128)} %bitcast.9), custom_call_target="tpu_custom_call" | custom-call | tf_op jit(solution)/shard_map/pallas_call | solution.py:520
  2.6 51.9 %all_to_all.20.refs_0_ = bf16[16,400,128]{2,1,0:T(8,128)(2,1)S(1)} all-to-all(bf16[16,400,128]{2,1,0:T(8,128)(2,1)} %shard_map.82), channel_id=1, replica_groups=mesh['seq'=32,'mem'=16] {'mem'}, dimensions={0} | all-to-all | bytes 3276800 | tf_op jit(solution)/shard_map/all_to_all | solution.py:521
  54.5 0.0 copy-done.3
  54.5 3.3 %shard_map.83 = (bf16[16,384,256]{2,1,0:T(8,128)(2,1)}, bf16[32,80,128]{2,1,0:T(8,128)(2,1)}) custom-call(bf16[16,400,128]{2,1,0:T(8,128)(2,1)S(1)} %all_to_all.20.refs_0_, bf16[16,16]{1,0:T(8,128)(2,1)S(1)} %copy-done.3), custom_call_target="tpu_custom_call" | custom-call | tf_op jit(solution)/shard_map/pallas_call | solution.py:522
  57.9 11.0 %all-to-all-start.1 = ((bf16[32,80,128]{2,1,0:T(8,128)(2,1)}), bf16[32,80,128]{2,1,0:T(8,128)(2,1)S(1)}, u32[]{:S(2)}, u32[]{:S(2)}) async-start(bf16[32,80,128]{2,1,0:T(8,128)(2,1)} %get-tuple-element.12), calls=%async_computation.1 | async-start | bytes 1310720 | tf_op jit(solution)/shard_map/all_to_all | solution.py:523
  68.9 12.0 %shard_map.84 = (f32[16,384,128]{2,1,0:T(8,128)}, bf16[32,384,128]{2,1,0:T(8,128)(2,1)}) custom-call(bf16[16,400,128]{2,1,0:T(8,128)(2,1)S(1)} %all_to_all.20.refs_0_, bf16[16,384,256]{2,1,0:T(8,128)(2,1)} %get-tuple-element.13.refs_1_, bf16[16,16]{1,0:T(8,128)(2,1)S(1)} %copy-done.3), custom_call_target="tpu_custom_call" | custom-call | flops 15000000512 | bytes 12582912 | tf_op jit(solution)/shard_map/pallas_call | solution.py:524
  80.9 7.0 %all-to-all-done.1.in_ref = bf16[32,80,128]{2,1,0:T(8,128)(2,1)S(1)} async-done(((bf16[32,80,128]{2,1,0:T(8,128)(2,1)}), bf16[32,80,128]{2,1,0:T(8,128)(2,1)S(1)}, u32[]{:S(2)}, u32[]{:S(2)}) %all-to-all-start.1) | async-done | bytes 655392 | tf_op jit(solution)/shard_map/all_to_all | solution.py:523
  87.9 0.0 copy-start
  87.9 0.0 copy-start.1
  87.9 0.0 copy-start.2
  87.9 0.2 shard_map.85
  88.1 20.7 %all_to_all.21 = bf16[32,64,128]{2,1,0:T(8,128)(2,1)S(1)} all-to-all(bf16[32,64,128]{2,1,0:T(8,128)(2,1)S(1)} %shard_map.85), channel_id=1, replica_groups=mesh['seq'=32,'mem'=16] {'seq'}, dimensions={0} | all-to-all | bytes 1048576 | tf_op jit(solution)/shard_map/all_to_all | solution.py:527
  108.8 0.0 copy-done
  108.8 0.0 copy-done.1
  108.8 0.0 copy-done.2
  108.8 1.9 %shard_map.86 = bf16[16,128,128]{2,1,0:T(8,128)(2,1)S(1)} custom-call(bf16[32,384,128]{2,1,0:T(8,128)(2,1)S(1)} %copy-done.1, f32[16,384,128]{2,1,0:T(8,128)S(1)} %copy-done, bf16[16,128,128]{2,1,0:T(8,128)(2,1)S(1)} %bitcast.5, f32[16,128]{1,0:T(8,128)S(1)} %bitcast.6), custom_call_target="tpu_custom_call" | custom-call | tf_op jit(solution)/shard_map/pallas_call | solution.py:529
  110.7 23.4 %all_to_all.22.in_ref = bf16[16,128,128]{2,1,0:T(8,128)(2,1)S(1)} all-to-all(bf16[16,128,128]{2,1,0:T(8,128)(2,1)S(1)} %shard_map.86), channel_id=1, replica_groups=mesh['seq'=32,'mem'=16] {'mem'}, dimensions={0} | all-to-all | bytes 1048576 | tf_op jit(solution)/shard_map/all_to_all | solution.py:530
  134.1 0.9 shard_map.87
Async XLA Ops:
  0.0 54.5 %copy-start.3 = (bf16[16,16]{1,0:T(8,128)(2,1)S(1)}, bf16[16,16]{1,0:T(8,128)(2,1)}, u32[]{:S(2)}) copy-start(bf16[16,16]{1,0:T(8,128)(2,1)} %refs_2_.3) | copy-start | bytes 1540
  57.9 30.0 %all-to-all-start.1 = ((bf16[32,80,128]{2,1,0:T(8,128)(2,1)}), bf16[32,80,128]{2,1,0:T(8,128)(2,1)S(1)}, u32[]{:S(2)}, u32[]{:S(2)}) async-start(bf16[32,80,128]{2,1,0:T(8,128)(2,1)} %get-tuple-element.12), calls=%async_computation.1 | async-start | bytes 1310720 | tf_op jit(solution)/shard_map/all_to_all | solution.py:523
  87.9 20.9 %copy-start = (f32[16,384,128]{2,1,0:T(8,128)S(1)}, f32[16,384,128]{2,1,0:T(8,128)}, u32[]{:S(2)}) copy-start(f32[16,384,128]{2,1,0:T(8,128)} %get-tuple-element.17.refs_1_) | copy-start | bytes 9437188
  87.9 20.9 %copy-start.1 = (bf16[32,384,128]{2,1,0:T(8,128)(2,1)S(1)}, bf16[32,384,128]{2,1,0:T(8,128)(2,1)}, u32[]{:S(2)}) copy-start(bf16[32,384,128]{2,1,0:T(8,128)(2,1)} %get-tuple-element.16.refs_0_) | copy-start | bytes 9437188
  87.9 20.9 %copy-start.2 = (f32[2048]{0:T(1024)S(1)}, f32[2048]{0:T(1024)}, u32[]{:S(2)}) copy-start(f32[2048]{0:T(1024)} %param.15) | copy-start | bytes 24580
